TPU v7x, 256 devices: a whole 4x4x8 slice. The times are simulated.
256 devices in a mesh: lat: 32 (over y, z_lo, x), lon: 8 (over z_hi, core).
Axes of the slice: x: 4, y: 4, z: 8 (z_hi: 4, z_lo: 2; z = z_hi * 2 + z_lo), core: 2. Of those that a mesh axis runs over, the one named last changes fastest.
Arguments:
- tracers: float32 [2, 32, 512, 2048], P(None, None, 'lat', 'lon'), may hold values from -12 to 12
- east_velocity: bfloat16 [32, 512, 2048], P(None, 'lat', 'lon'), may hold values from -6 to 6
- north_velocity: bfloat16 [32, 512, 2048], P(None, 'lat', 'lon'), may hold values from -6 to 6
- column_levels: int32 [512, 2048], P('lat', 'lon'), may hold values from 0 to 32
- surface_term: float32 [512, 2048], P('lat', 'lon'), may hold values from 0.05 to 2
Outputs:
- updated: float32 [2, 32, 512, 2048], P(None, None, 'lat', 'lon')
- gradient: float32 [2, 512, 2048], P(None, 'lat', 'lon')
Inputs may be any that keep to these rules, and one draw needn't show every extreme that they name: column_levels counts the ocean levels of a column; 0 is land.
All inputs are finite; a program needn't handle non-finite values.
Results may differ from a plain program's by a relative error of at most 0.0003.
Values may be sent and summed in bfloat16 or wider, within the bound.
A program may use at most 128 MiB of HBM per device.

v0:
```python
import math

import jax
import jax.numpy as jnp
from jax import lax
from jax.sharding import PartitionSpec as P

ITERS = 4


time_step = 0.5
biharm_coef = 0.05
vertical_coef = 0.8


def extended(cells, sides, width):
    for axis, dim in sides:
        count = lax.axis_size(axis)
        head = lax.slice_in_dim(cells, 0, width, axis=dim)
        tail = lax.slice_in_dim(cells, cells.shape[dim] - width, cells.shape[dim], axis=dim)
        cells = jnp.concatenate(
            [
                lax.ppermute(tail, axis, [(i, (i + 1) % count) for i in range(count)]),
                cells,
                lax.ppermute(head, axis, [((i + 1) % count, i) for i in range(count)]),
            ],
            axis=dim,
        )
    return cells


def fix_rims(padded, dim, width):
    index = lax.axis_index("lat")
    count = lax.axis_size("lat")
    height = padded.shape[dim]
    row_ids = jnp.arange(height)
    cut = (row_ids < width) & (index == 0) | (row_ids >= height - width) & (index == count - 1)
    shape_list = [1] * padded.ndim
    shape_list[dim] = height
    return jnp.where(cut.reshape(shape_list), jnp.zeros((), padded.dtype), padded)


def pieces(grid):
    return (
        grid[..., 1:-1, 1:-1],
        grid[..., 1:-1, 2:],
        grid[..., 1:-1, :-2],
        grid[..., 2:, 1:-1],
        grid[..., :-2, 1:-1],
    )


def laplace_pad(grid, ocean):
    values = pieces(grid)
    masks = pieces(ocean)
    center = values[0]
    total = masks[1] * (values[1] - center) + masks[2] * (values[2] - center)
    total = total + masks[3] * (values[3] - center) + masks[4] * (values[4] - center)
    return masks[0] * total


def transport_pad(grid, ocean, eastward, northward):
    values = pieces(grid)
    masks = pieces(ocean)
    speed_east = pieces(eastward)
    speed_north = pieces(northward)
    east_flux = speed_east[0] * masks[0] * masks[1] * (values[0] + values[1]) * 0.5
    west_flux = speed_east[2] * masks[2] * masks[0] * (values[2] + values[0]) * 0.5
    north_flux = speed_north[0] * masks[0] * masks[3] * (values[0] + values[3]) * 0.5
    south_flux = speed_north[4] * masks[4] * masks[0] * (values[4] + values[0]) * 0.5
    return -(east_flux - west_flux) - (north_flux - south_flux)


def level_up(field):
    return jnp.concatenate([field[..., 1:, :, :], jnp.zeros_like(field[..., :1, :, :])], axis=-3)


def level_down(field):
    return jnp.concatenate([jnp.zeros_like(field[..., :1, :, :]), field[..., :-1, :, :]], axis=-3)


def vertical(field, ocean):
    return ocean * (
        level_up(ocean) * (level_up(field) - field)
        + level_down(ocean) * (level_down(field) - field)
    )


def tendency_pad(grid, ocean_two, eastward, northward):
    inner = grid[..., 1:-1, 1:-1]
    ocean_one = ocean_two[..., 1:-1, 1:-1]
    ocean_zero = ocean_one[..., 1:-1, 1:-1]
    center = inner[..., 1:-1, 1:-1]
    smooth = laplace_pad(laplace_pad(grid, ocean_two), ocean_one)
    moved = transport_pad(inner, ocean_one, eastward, northward)
    return ocean_zero * (
        moved - biharm_coef * smooth + vertical_coef * vertical(center, ocean_zero)
    )


def tracer_ext(field):
    return fix_rims(extended(field, (("lat", 2), ("lon", 3)), 2), 2, 2)


def nine_point(padded, surface, diagonal):
    center = padded[1:-1, 1:-1]
    edges = surface[1:-1, 2:] * padded[1:-1, 2:] + surface[1:-1, :-2] * padded[1:-1, :-2]
    edges = edges + surface[2:, 1:-1] * padded[2:, 1:-1] + surface[:-2, 1:-1] * padded[:-2, 1:-1]
    corners = surface[2:, 2:] * padded[2:, 2:] + surface[2:, :-2] * padded[2:, :-2]
    corners = corners + surface[:-2, 2:] * padded[:-2, 2:] + surface[:-2, :-2] * padded[:-2, :-2]
    return diagonal * center - surface[1:-1, 1:-1] * (edges + 0.5 * corners)


def slope(padded, surface):
    values = pieces(padded)
    masks = pieces(surface)
    east_slope = masks[0] * masks[1] * (values[1] - values[0])
    north_slope = masks[0] * masks[3] * (values[3] - values[0])
    return jnp.stack([east_slope, north_slope])


def solve(forcing, diagonal, surface, padder, totals):
    pressure = jnp.zeros_like(forcing)
    resid = forcing
    precond = resid / diagonal
    direction = precond
    product_now = totals(jnp.stack([jnp.sum(resid * precond)]))[0]
    for iteration in range(ITERS):
        image = nine_point(padder(direction), surface, diagonal)
        alpha = product_now / totals(jnp.stack([jnp.sum(direction * image)]))[0]
        pressure = pressure + alpha * direction
        resid = resid - alpha * image
        if iteration + 1 < ITERS:
            precond = resid / diagonal
            product_next = totals(jnp.stack([jnp.sum(resid * precond)]))[0]
            direction = precond + product_next / product_now * direction
            product_now = product_next
    return pressure


def body(tracers, east_velocity, north_velocity, column_levels, surface_term):
    levels = tracers.shape[1]
    stacked = jnp.concatenate(
        [east_velocity, north_velocity, column_levels.astype(jnp.bfloat16)[None]], axis=0
    )
    flow = fix_rims(extended(stacked, (("lat", 1), ("lon", 2)), 2), 1, 2)
    eastward = flow[:levels, 1:-1, 1:-1].astype(jnp.float32)
    northward = flow[levels : 2 * levels, 1:-1, 1:-1].astype(jnp.float32)
    depth_ext = flow[2 * levels].astype(jnp.float32)
    ocean_two = (jnp.arange(levels, dtype=jnp.float32)[:, None, None] < depth_ext[None]).astype(
        jnp.float32
    )
    first = tendency_pad(tracer_ext(tracers), ocean_two, eastward, northward)
    middle = tracers + time_step * first
    second = tendency_pad(tracer_ext(middle), ocean_two, eastward, northward)
    updated = tracers + 0.5 * time_step * (first + second)
    ocean_zero = ocean_two[:, 2:-2, 2:-2]
    surface_one = (depth_ext[1:-1, 1:-1] > 0).astype(jnp.float32)
    forcing = jnp.sum(ocean_zero * (updated[0] - 0.5 * updated[1]), axis=0) / math.sqrt(levels)
    diagonal = 6.0 + surface_term

    def padder(field):
        return fix_rims(extended(field, (("lat", 0), ("lon", 1)), 1), 0, 1)

    def totals(local):
        return lax.psum(local, ("lat", "lon"))

    pressure = solve(forcing, diagonal, surface_one, padder, totals)
    gradient = slope(padder(pressure), surface_one)
    return (updated, gradient)


def solution(mesh):
    in_specs = (
        P(None, None, "lat", "lon"),
        P(None, "lat", "lon"),
        P(None, "lat", "lon"),
        P("lat", "lon"),
        P("lat", "lon"),
    )
    out_specs = (P(None, None, "lat", "lon"), P(None, "lat", "lon"))
    return jax.shard_map(body, mesh=mesh, in_specs=in_specs, out_specs=out_specs, check_vma=False)
```

profile of v0, /device:TPU:1, one launch (start us, length us, event | category | flops | bytes accessed | tf_op | source)
XLA Modules:
  0.0 723.7 jit_solution(12336076632863453007)
XLA Ops:
  4.8 5.2 collective-permute-start.1
  11.9 5.7 collective-permute-start.5
  19.3 4.5 collective-permute-start.2
  23.8 6.6 collective-permute-done.2
  35.6 3.4 fusion.132
  39.0 3.3 fusion.75
  65.7 3.5 multiply_add_fusion
  69.4 5.7 collective-permute-start.9
  95.6 3.9 fusion.2
  104.6 6.1 collective-permute-start.13
  118.8 81.8 %all-reduce.6 = (f32[1]{0:T(128)}, f32[1]{0:T(128)}) all-reduce(f32[1]{0:T(128)} %bitcast.3, f32[1]{0:T(128)} %bitcast.4), channel_id=1, replica_groups=mesh['lat'=32,'lon'=8] {'lat','lon'}, use_global_device_ids=true, to_apply=%region_2.3 | all-reduce | flops 2 | bytes 16 | tf_op jit(solution)/shard_map/psum | solution.py:166
  202.6 72.7 %psum.58 = f32[1]{0:T(128)} all-reduce(f32[1]{0:T(128)} %bitcast.6), channel_id=1, replica_groups=mesh['lat'=32,'lon'=8] {'lat','lon'}, use_global_device_ids=true, to_apply=%region_6.7 | all-reduce | flops 1 | bytes 8 | tf_op jit(solution)/shard_map/psum | solution.py:166
  276.7 6.0 collective-permute-start.17
  286.1 3.2 collective-permute-done.19
  290.1 80.1 %psum.59 = f32[1]{0:T(128)} all-reduce(f32[1]{0:T(128)} %bitcast.8), channel_id=1, replica_groups=mesh['lat'=32,'lon'=8] {'lat','lon'}, use_global_device_ids=true, to_apply=%region_8.9 | all-reduce | flops 1 | bytes 8 | tf_op jit(solution)/shard_map/psum | solution.py:166
  372.1 72.4 %psum.60 = f32[1]{0:T(128)} all-reduce(f32[1]{0:T(128)} %bitcast.10), channel_id=1, replica_groups=mesh['lat'=32,'lon'=8] {'lat','lon'}, use_global_device_ids=true, to_apply=%region_10.11 | all-reduce | flops 1 | bytes 8 | tf_op jit(solution)/shard_map/psum | solution.py:166
  446.4 5.2 collective-permute-start.21
  459.2 79.9 %psum.61 = f32[1]{0:T(128)} all-reduce(f32[1]{0:T(128)} %bitcast.12), channel_id=1, replica_groups=mesh['lat'=32,'lon'=8] {'lat','lon'}, use_global_device_ids=true, to_apply=%region_12.13 | all-reduce | flops 1 | bytes 8 | tf_op jit(solution)/shard_map/psum | solution.py:166
  541.1 72.5 %psum.62 = f32[1]{0:T(128)} all-reduce(f32[1]{0:T(128)} %bitcast.14), channel_id=1, replica_groups=mesh['lat'=32,'lon'=8] {'lat','lon'}, use_global_device_ids=true, to_apply=%region_14.15 | all-reduce | flops 1 | bytes 8 | tf_op jit(solution)/shard_map/psum | solution.py:166
  615.4 5.3 collective-permute-start.25
  624.2 3.2 collective-permute-done.27
  628.3 79.9 %psum.63 = f32[1]{0:T(128)} all-reduce(f32[1]{0:T(128)} %bitcast.16), channel_id=1, replica_groups=mesh['lat'=32,'lon'=8] {'lat','lon'}, use_global_device_ids=true, to_apply=%region_16.17 | all-reduce | flops 1 | bytes 8 | tf_op jit(solution)/shard_map/psum | solution.py:166
  709.7 5.7 collective-permute-start.29
  719.5 3.2 collective-permute-done.31
  (196 shorter events, 94.3 us)
Async XLA Ops:
  2.6 15.0 %collective-permute-start = (bf16[65,2,256]{2,1,0:T(2,128)(2,1)S(1)}, bf16[65,2,256]{2,1,0:T(2,128)(2,1)S(1)}, u32[]{:S(2)}, u32[]{:S(2)}) collective-permute-start(bf16[65,2,256]{2,1,0:T(2,128)(2,1)S(1)} %get-tuple-element.55), channel_id=1, source_target_pairs={{0,8},{8,16},{16,24},{24,32},{32,40},{40,48},{48,56},{56,64},{64,7... | collective-permute-start | bytes 199688 | tf_op jit(solution)/shard_map/ppermute | solution.py:23
  4.8 12.8 %collective-permute-start.1 = (bf16[65,2,256]{2,1,0:T(2,128)(2,1)S(1)}, bf16[65,2,256]{2,1,0:T(2,128)(2,1)S(1)}, u32[]{:S(2)}, u32[]{:S(2)}) collective-permute-start(bf16[65,2,256]{2,1,0:T(2,128)(2,1)S(1)} %get-tuple-element.56), channel_id=1, source_target_pairs={{8,0},{16,8},{24,16},{32,24},{40,32},{48,40},{56,48},{64,56},{72,6... | collective-permute-start | bytes 199688 | tf_op jit(solution)/shard_map/ppermute | solution.py:25
  11.9 30.4 %collective-permute-start.4 = (f32[2,32,2,256]{3,2,1,0:T(2,128)}, f32[2,32,2,256]{3,2,1,0:T(2,128)}, u32[]{:S(2)}, u32[]{:S(2)}) collective-permute-start(f32[2,32,2,256]{3,2,1,0:T(2,128)} %get-tuple-element.51), channel_id=1, source_target_pairs={{0,8},{8,16},{16,24},{24,32},{32,40},{40,48},{48,56},{56,64},{64,7... | collective-permute-start | bytes 393224 | tf_op jit(solution)/shard_map/ppermute | solution.py:23
  11.9 30.4 %collective-permute-start.5 = (f32[2,32,2,256]{3,2,1,0:T(2,128)}, f32[2,32,2,256]{3,2,1,0:T(2,128)}, u32[]{:S(2)}, u32[]{:S(2)}) collective-permute-start(f32[2,32,2,256]{3,2,1,0:T(2,128)} %get-tuple-element.52), channel_id=1, source_target_pairs={{8,0},{16,8},{24,16},{32,24},{40,32},{48,40},{56,48},{64,56},{72,6... | collective-permute-start | bytes 393224 | tf_op jit(solution)/shard_map/ppermute | solution.py:25
  19.3 11.1 %collective-permute-start.2 = (bf16[65,20,2]{2,1,0:T(8,128)(2,1)S(1)}, bf16[65,20,2]{2,1,0:T(8,128)(2,1)S(1)}, u32[]{:S(2)}, u32[]{:S(2)}) collective-permute-start(bf16[65,20,2]{2,1,0:T(8,128)(2,1)S(1)} %get-tuple-element.53), channel_id=1, source_target_pairs={{0,1},{1,2},{2,3},{3,4},{4,5},{5,6},{6,7},{7,0},{8,9},{9,10},{10,1... | collective-permute-start | bytes 15608 | tf_op jit(solution)/shard_map/ppermute | solution.py:23
  23.8 9.5 %collective-permute-start.3 = (bf16[65,20,2]{2,1,0:T(8,128)(2,1)S(1)}, bf16[65,20,2]{2,1,0:T(8,128)(2,1)S(1)}, u32[]{:S(2)}, u32[]{:S(2)}) collective-permute-start(bf16[65,20,2]{2,1,0:T(8,128)(2,1)S(1)} %get-tuple-element.54), channel_id=1, source_target_pairs={{1,0},{2,1},{3,2},{4,3},{5,4},{6,5},{7,6},{0,7},{9,8},{10,9},{11,1... | collective-permute-start | bytes 15608 | tf_op jit(solution)/shard_map/ppermute | solution.py:25
  46.4 7.3 %collective-permute-start.6 = (f32[2,32,20,2]{1,2,3,0:T(8,128)S(1)}, f32[2,32,20,2]{1,2,3,0:T(8,128)}, u32[]{:S(2)}, u32[]{:S(2)}) collective-permute-start(f32[2,32,20,2]{1,2,3,0:T(8,128)S(1)} %copy.18), channel_id=1, source_target_pairs={{0,1},{1,2},{2,3},{3,4},{4,5},{5,6},{6,7},{7,0},{8,9},{9,10},{10,1... | collective-permute-start | bytes 30728 | tf_op jit(solution)/shard_map/ppermute | solution.py:23
  49.3 6.5 collective-permute-start.7
  69.3 8.1 %collective-permute-start.8 = (f32[2,32,2,256]{3,2,1,0:T(2,128)S(1)}, f32[2,32,2,256]{3,2,1,0:T(2,128)S(1)}, u32[]{:S(2)}, u32[]{:S(2)}) collective-permute-start(f32[2,32,2,256]{3,2,1,0:T(2,128)S(1)} %get-tuple-element.49), channel_id=1, source_target_pairs={{0,8},{8,16},{16,24},{24,32},{32,40},{40,48},{48,56},{56,64},{64,7... | collective-permute-start | bytes 393224 | tf_op jit(solution)/shard_map/ppermute | solution.py:23
  69.4 8.0 %collective-permute-start.9 = (f32[2,32,2,256]{3,2,1,0:T(2,128)S(1)}, f32[2,32,2,256]{3,2,1,0:T(2,128)S(1)}, u32[]{:S(2)}, u32[]{:S(2)}) collective-permute-start(f32[2,32,2,256]{3,2,1,0:T(2,128)S(1)} %get-tuple-element.50), channel_id=1, source_target_pairs={{8,0},{16,8},{24,16},{32,24},{40,32},{48,40},{56,48},{64,56},{72,6... | collective-permute-start | bytes 393224 | tf_op jit(solution)/shard_map/ppermute | solution.py:25
  80.6 7.4 %collective-permute-start.10 = (f32[2,32,20,2]{1,2,3,0:T(8,128)S(1)}, f32[2,32,20,2]{1,2,3,0:T(8,128)}, u32[]{:S(2)}, u32[]{:S(2)}) collective-permute-start(f32[2,32,20,2]{1,2,3,0:T(8,128)S(1)} %copy.22), channel_id=1, source_target_pairs={{0,1},{1,2},{2,3},{3,4},{4,5},{5,6},{6,7},{7,0},{8,9},{9,10},{10,1... | collective-permute-start | bytes 30728 | tf_op jit(solution)/shard_map/ppermute | solution.py:23
  85.2 5.2 collective-permute-start.11
  104.5 7.1 collective-permute-start.12
  104.6 7.0 collective-permute-start.13
  111.7 4.9 collective-permute-start.14
  112.9 5.1 collective-permute-start.15
  276.6 6.7 collective-permute-start.16
  276.7 6.7 collective-permute-start.17
  445.9 6.7 collective-permute-start.20
  446.4 6.2 collective-permute-start.21
  614.9 6.7 collective-permute-start.24
  615.4 6.2 collective-permute-start.25
  709.5 6.9 collective-permute-start.28
  709.7 6.6 collective-permute-start.29
  (46 other events, 826.6 us)
where the time goes:
time: 734 us; the launch traced here: 724 us
  blocking collectives  539 us (73%)
  starting transfers between devices  73.9 us (10%)
  other arithmetic  36 us (5%)
  waiting for transfers between devices  33.8 us (5%)
  local copies, waits for them, and re-layouts  30.2 us (4%)
  between operations  10.6 us (1%)
    psum x7, blocking collectives, totals(): return lax.psum(local, ('lat', 'lon'))  539 us
    ppermute x16, starting transfers between devices, extended(): lax.ppermute(head, axis, [((i + 1) % count, i) for i in range(count)])  53.9 us
    ppermute x16, starting transfers between devices, extended(): lax.ppermute(tail, axis, [(i, (i + 1) % count) for i in range(count)])  19.9 us
    ppermute x16, waiting for transfers between devices, extended(): lax.ppermute(head, axis, [((i + 1) % count, i) for i in range(count)])  17.7 us
    ppermute x16, waiting for transfers between devices, extended(): lax.ppermute(tail, axis, [(i, (i + 1) % count) for i in range(count)])  16.1 us
  transfers between devices with their start and end apart: 32, of which 20 were waited for; matrix products, arithmetic and copies ran while one was open for 3% of the time, Pallas kernels for 0%

commit v1 on v0

v1 whole, which is shorter than its diff:
```python
import functools
import math

import jax
import jax.numpy as jnp
from jax import lax
from jax.experimental import pallas as pl
from jax.experimental.pallas import tpu as pltpu
from jax.sharding import PartitionSpec as P

MESH = pl.DeviceIdType.MESH
F32 = jnp.float32
BF16 = jnp.bfloat16

ITERS = 4
LEVELS = 32
ROWS = 16
HALO = 4
HIGH = ROWS + 2 * HALO
NX = 4
NZ = 2

time_step = 0.5
biharm_coef = 0.05
vertical_coef = 0.8


def iota(shape, axis):
    return lax.broadcasted_iota(jnp.int32, shape, axis)


def kernel(
    lats, lons, trc, vel_e, vel_n, levels_in, term_in, upd, grad,
    tin, vin, vf, levi, termi, X, M, LP, V, Xs, Ms, LPs, Us, Vs, Qt, Qv, pack, pack_in, corner_in,
    xb, xb_in, vbn, vbs, vbn_in, vbs_in, FL, frn, frs, fre, frw, fc,
    FO, gn, gs, ge, gw, gc, MK, FS, tout, sa, ra, sb, rb,
    in_sem, out_sem, s1, r1, s2, r2, sas, sar, sbs, sbr,
):
    la, lo = lax.axis_index("lat"), lax.axis_index("lon")
    north, south = lax.rem(la + 1, lats), lax.rem(la + lats - 1, lats)
    east, west = lax.rem(lo + 1, lons), lax.rem(lo + lons - 1, lons)
    ny = lats // (NX * NZ)
    y, zx = la // (NX * NZ), lax.rem(la, NX * NZ)
    zz, xx = zx // NX, lax.rem(zx, NX)
    size_a, size_b = ny * NX, NZ * lons
    me_a, me_b = y * NX + xx, zz * lons + lo

    def partner_a(k):
        a = lax.rem(me_a + k, size_a)
        return ((a // NX) * NZ + zz) * NX + lax.rem(a, NX), lo

    def partner_b(k):
        b = lax.rem(me_b + k, size_b)
        return (y * NZ + b // lons) * NX + xx, lax.rem(b, lons)

    loads = []
    for h in range(2):
        loads.append(pltpu.make_async_copy(trc.at[:, pl.ds(128 * h, 128)], tin.at[h], in_sem.at[h]))
    for w, src in enumerate((vel_e, vel_n)):
        for h in range(2):
            loads.append(pltpu.make_async_copy(src.at[:, pl.ds(128 * h, 128)], vin.at[w, h], in_sem.at[2 + 2 * w + h]))
    loads.append(pltpu.make_async_copy(levels_in, levi, in_sem.at[6]))
    loads.append(pltpu.make_async_copy(term_in, termi, in_sem.at[7]))
    for load in loads:
        load.start()

    barrier = pltpu.get_barrier_semaphore()
    around = [
        (north, lo), (south, lo), (la, east), (la, west),
        (north, east), (south, east), (north, west), (south, west),
    ]
    partners = [partner_a(k) for k in range(1, size_a)] + [partner_b(k) for k in range(1, size_b)]
    for device in around + partners:
        pl.semaphore_signal(barrier, inc=1, device_id=device, device_id_type=MESH)

    def send(src, dst, k, device, ss=s1, rr=r1):
        copy = pltpu.make_async_remote_copy(
            src_ref=src, dst_ref=dst, send_sem=ss.at[k], recv_sem=rr.at[k], device_id=device, device_id_type=MESH
        )
        copy.start()
        return copy

    lane = iota((8, 128), 1)
    sub = iota((8, 128), 0)
    lane16 = lax.rem(lane, 16)
    laneq = lane // 16

    loads[0].wait()
    loads[1].wait()

    def fill_x(r, carry):
        for h in range(2):
            X[r + HALO, h] = tin[h, pl.ds(r, 64, stride=ROWS), :]
        return carry

    lax.fori_loop(0, ROWS, fill_x, 0)
    for j in range(2):
        xb[0, j] = X[16 + j].astype(BF16)
        xb[1, j] = X[6 + j].astype(BF16)

    loads[6].wait()
    loads[7].wait()
    for h in range(2):
        for tile in range(2):
            FL[h, tile, 0] = levi[8 * tile : 8 * tile + 8, 128 * h : 128 * h + 128].astype(F32)
            FL[h, tile, 1] = termi[8 * tile : 8 * tile + 8, 128 * h : 128 * h + 128]

    pl.semaphore_wait(barrier, len(around) + len(partners))

    c_rows = [
        send(X.at[pl.ds(18, 2)], X.at[pl.ds(2, 2)], 0, (north, lo)),
        send(X.at[pl.ds(4, 2)], X.at[pl.ds(20, 2)], 2, (south, lo)),
        send(xb.at[0], xb_in.at[0], 1, (north, lo)),
        send(xb.at[1], xb_in.at[1], 3, (south, lo)),
    ]
    c_flat = [
        send(FL.at[:, 1], frs, 13, (north, lo)),
        send(FL.at[:, 0], frn, 14, (south, lo)),
        send(FL.at[1], frw, 15, (la, east)),
        send(FL.at[0], fre, 16, (la, west)),
        send(FL.at[1, 1], fc.at[0], 17, (north, east)),
        send(FL.at[1, 0], fc.at[1], 18, (south, east)),
        send(FL.at[0, 1], fc.at[2], 19, (north, west)),
        send(FL.at[0, 0], fc.at[3], 20, (south, west)),
    ]

    for load in loads[2:6]:
        load.wait()

    def widen(n, carry):
        at = pl.ds(pl.multiple_of(64 * n, 64), 64)
        for w in range(2):
            for h in range(2):
                vf[w, h, at, :] = vin[w, h, at, :].astype(F32) * 0.5
        return carry

    lax.fori_loop(0, 8, widen, 0)

    def fill_v(r, carry):
        for w in range(2):
            for h in range(2):
                V[r + HALO, w, h] = vf[w, h, pl.ds(r, 32, stride=ROWS), :]
        return carry

    lax.fori_loop(0, ROWS, fill_v, 0)
    for j in range(3):
        vbn[j] = V[17 + j].astype(BF16)
    for j in range(2):
        vbs[j] = V[4 + j].astype(BF16)
    c_vel = [
        send(vbn.at[pl.ds(1, 2)], vbn_in.at[pl.ds(1, 2)], 4, (north, lo)),
        send(vbn.at[0, 1], vbn_in.at[0, 1], 5, (north, lo)),
        send(vbs, vbs_in, 6, (south, lo)),
    ]

    def seam_of(parts):
        out = jnp.zeros((8, 128), F32)
        for q, (low, high) in enumerate(parts):
            both = jnp.where(lane >= 124, high, low)
            out = jnp.where(laneq == q, pltpu.roll(both, (16 * q + 4) % 128, 1), out)
        return out

    def seam_x(i):
        return seam_of([(X[i, 0, 8 * q : 8 * q + 8, :], X[i, 1, 8 * q : 8 * q + 8, :]) for q in range(8)])

    def seam_v(i):
        return seam_of(
            [
                (V[i, q // 4, 0, 8 * (q % 4) : 8 * (q % 4) + 8, :], V[i, q // 4, 1, 8 * (q % 4) : 8 * (q % 4) + 8, :])
                for q in range(8)
            ]
        )

    def pack_rows(r, carry):
        Qt[r] = seam_x(r + HALO)
        Qv[r] = seam_v(r + HALO)
        return carry

    lax.fori_loop(0, ROWS, pack_rows, 0)
    for a in range(4):
        for w, Q in enumerate((Qt, Qv)):
            for side in range(2):
                out = jnp.zeros((8, 128), F32)
                for n in range(4):
                    turn = (4 * n - 4 * side) % 128
                    out = jnp.where(lane16 // 4 == n, pltpu.roll(Q[4 * a + n], turn, 1) if turn else Q[4 * a + n], out)
                pack[side, a, w] = out
    c_seam = [
        send(pack.at[0], pack_in.at[0], 7, (la, east)),
        send(pack.at[1], pack_in.at[1], 8, (la, west)),
        send(pack.at[0, 3], corner_in.at[0], 9, (north, east)),
        send(pack.at[0, 0], corner_in.at[1], 10, (south, east)),
        send(pack.at[1, 3], corner_in.at[2], 11, (north, west)),
        send(pack.at[1, 0], corner_in.at[3], 12, (south, west)),
    ]

    def flat(own, n, s, e, w, ne, se, nw, sw):
        parts = [jnp.concatenate([own[h][0], own[h][1], jnp.where(sub < 4, n[h], s[h])], axis=0) for h in range(2)]
        right = jnp.concatenate([e[0], e[1], jnp.where(sub < 4, ne, se)], axis=0)
        left = jnp.concatenate([w[0], w[1], jnp.where(sub < 4, nw, sw)], axis=0)
        parts.append(jnp.where(iota((24, 128), 1) < 64, right, left))
        return parts

    def to_east(parts):
        rolled = [pltpu.roll(p, 127, 1) for p in parts]
        last = iota(parts[0].shape, 1) == 127
        return [jnp.where(last, rolled[(k + 1) % 3], rolled[k]) for k in range(3)]

    def to_west(parts):
        rolled = [pltpu.roll(p, 1, 1) for p in parts]
        first = iota(parts[0].shape, 1) == 0
        return [jnp.where(first, rolled[(k + 2) % 3], rolled[k]) for k in range(3)]

    def to_north(part):
        return pltpu.roll(part, 23, 0)

    def to_south(part):
        return pltpu.roll(part, 1, 0)

    for copy in c_flat:
        copy.wait()

    def flat_field(f):
        return flat(
            [[FL[h, tile, f] for tile in range(2)] for h in range(2)],
            [frn[h, f] for h in range(2)], [frs[h, f] for h in range(2)],
            [fre[tile, f] for tile in range(2)], [frw[tile, f] for tile in range(2)],
            fc[3, f], fc[2, f], fc[1, f], fc[0, f],
        )

    row = iota((24, 128), 0)
    past_north = jnp.logical_and(row >= 16, row < 20).astype(jnp.int32) * (la == lats - 1).astype(jnp.int32)
    past_south = (row >= 20).astype(jnp.int32) * (la == 0).astype(jnp.int32)
    outside = (past_north + past_south) > 0
    depth = [jnp.where(outside, 0.0, p) for p in flat_field(0)]
    diagonal = [6.0 + p for p in flat_field(1)]

    wide = iota((24, 128), 1)
    seam_e = jnp.where(wide >= 124, depth[1], depth[2])
    seam_w = jnp.where(wide >= 124, depth[2], depth[0])
    base = jnp.where(wide < 8, pltpu.roll(seam_e, 4, 1), pltpu.roll(seam_w, 12, 1))
    base = jnp.where(wide < 16, base, 0.0)
    for turn in (16, 32, 64):
        base = base + pltpu.roll(base, turn, 1)
    east_depth = to_east(depth) + [pltpu.roll(base, 127, 1)]
    west_depth = to_west(depth) + [pltpu.roll(base, 1, 1)]
    for slot, p in enumerate((0, 1, 3)):
        own = (depth + [base])[p]
        MK[slot, 0] = own
        MK[slot, 1] = jnp.minimum(own, east_depth[p])
        MK[slot, 2] = jnp.minimum(own, west_depth[p])
        MK[slot, 3] = jnp.minimum(own, to_north(own))
        MK[slot, 4] = jnp.minimum(own, to_south(own))

    for copy in c_rows + c_vel + c_seam:
        copy.wait()
    for j in range(2):
        X[j] = xb_in[0, j].astype(F32)
        X[22 + j] = xb_in[1, j].astype(F32)
        V[2 + j] = vbn_in[1 + j].astype(F32)
        V[20 + j] = vbs_in[j].astype(F32)
    V[1, 1] = vbn_in[0, 1].astype(F32)

    def seam_row(own, from_east, from_west, n):
        out = jnp.where(lane16 < 4, own, pltpu.roll(own, 8, 1))
        right = pltpu.roll(from_east, (4 - 4 * n) % 128, 1) if n != 1 else from_east
        left = pltpu.roll(from_west, (8 - 4 * n) % 128, 1) if n != 2 else from_west
        out = jnp.where(lane16 // 4 == 1, right, out)
        return jnp.where(lane16 // 4 == 2, left, out)

    def put_velocity(i, both):
        other = pltpu.roll(both, 64, 1)
        Us[i] = jnp.where(lane < 64, both, other)
        Vs[i] = jnp.where(lane < 64, other, both)

    for a in range(4):
        for n in range(4):
            i = HALO + 4 * a + n
            Xs[i] = seam_row(Qt[4 * a + n], pack_in[1, a, 0], pack_in[0, a, 0], n)
            put_velocity(i, seam_row(Qv[4 * a + n], pack_in[1, a, 1], pack_in[0, a, 1], n))
    for n in range(4):
        Xs[n] = seam_row(seam_x(n), corner_in[2, 0], corner_in[0, 0], n)
        Xs[20 + n] = seam_row(seam_x(20 + n), corner_in[3, 0], corner_in[1, 0], n)
        if n > 0:
            put_velocity(n, seam_row(seam_v(n), corner_in[2, 1], corner_in[0, 1], n))
        if n < 2:
            put_velocity(20 + n, seam_row(seam_v(20 + n), corner_in[3, 1], corner_in[1, 1], n))

    level = iota((LEVELS, 128), 0).astype(F32)
    level_s = (sub + 8 * lax.rem(laneq, 4)).astype(F32)
    lane_f = iota((LEVELS, 128), 1)

    def mask_row(slot, n, i):
        return MK[slot, n, pl.ds(lax.rem(i + 20, 24), 1), :]

    def pull(seam, t, src, dst):
        return jnp.concatenate(
            [pltpu.roll(seam, (dst - 16 * (4 * t + g) - src) % 128, 1) for g in range(4)], axis=0
        )

    def shift_e(halves, seam, t):
        low, high = pltpu.roll(halves[0], 127, 1), pltpu.roll(halves[1], 127, 1)
        return [jnp.where(lane_f == 127, high, low), jnp.where(lane_f == 127, pull(seam, t, 4, 127), high)]

    def shift_w(halves, seam, t):
        low, high = pltpu.roll(halves[0], 1, 1), pltpu.roll(halves[1], 1, 1)
        return [jnp.where(lane_f == 0, pull(seam, t, 11, 0), low), jnp.where(lane_f == 0, low, high)]

    def at(ref, i, h, t):
        return ref[i, h, 32 * t : 32 * t + 32, :]

    def laplace(ref, seams, first, last):
        def step(i, carry):
            seam = seams[i]
            for t in range(2):
                x = [at(ref, i, h, t) for h in range(2)]
                xe, xw = shift_e(x, seam, t), shift_w(x, seam, t)
                for h in range(2):
                    total = jnp.where(level < mask_row(h, 1, i), xe[h] - x[h], 0.0)
                    total += jnp.where(level < mask_row(h, 2, i), xw[h] - x[h], 0.0)
                    total += jnp.where(level < mask_row(h, 3, i), at(ref, i + 1, h, t) - x[h], 0.0)
                    total += jnp.where(level < mask_row(h, 4, i), at(ref, i - 1, h, t) - x[h], 0.0)
                    LP[i, h, 32 * t : 32 * t + 32, :] = total
            total = jnp.where(level_s < mask_row(2, 1, i), pltpu.roll(seam, 127, 1) - seam, 0.0)
            total += jnp.where(level_s < mask_row(2, 2, i), pltpu.roll(seam, 1, 1) - seam, 0.0)
            total += jnp.where(level_s < mask_row(2, 3, i), seams[i + 1] - seam, 0.0)
            total += jnp.where(level_s < mask_row(2, 4, i), seams[i - 1] - seam, 0.0)
            LPs[i] = total
            return carry

        lax.fori_loop(first, last, step, 0)

    def north_flux(ref, seams, i):
        flux = []
        for t in range(2):
            for h in range(2):
                value = V[i, 1, h] * (at(ref, i, h, t) + at(ref, i + 1, h, t))
                value += biharm_coef * (at(LP, i + 1, h, t) - at(LP, i, h, t))
                flux.append(jnp.where(level < mask_row(h, 3, i), value, 0.0))
        value = Vs[i] * (seams[i] + seams[i + 1]) + biharm_coef * (LPs[i + 1] - LPs[i])
        flux.append(jnp.where(level_s < mask_row(2, 3, i), value, 0.0))
        return flux

    def tendency(ref, seams, first, last, put, put_seam):
        def step(i, below):
            above = north_flux(ref, seams, i)
            seam = seams[i]
            value = Us[i] * (seam + pltpu.roll(seam, 127, 1)) + biharm_coef * (pltpu.roll(LPs[i], 127, 1) - LPs[i])
            flux_s = jnp.where(level_s < mask_row(2, 1, i), value, 0.0)
            for t in range(2):
                x = [at(ref, i, h, t) for h in range(2)]
                lap = [at(LP, i, h, t) for h in range(2)]
                xe, lape = shift_e(x, seam, t), shift_e(lap, LPs[i], t)
                flux = []
                for h in range(2):
                    value = V[i, 0, h] * (x[h] + xe[h]) + biharm_coef * (lape[h] - lap[h])
                    flux.append(jnp.where(level < mask_row(h, 1, i), value, 0.0))
                flux_w = shift_w(flux, flux_s, t)
                for h in range(2):
                    up = jnp.where(level + 1.0 < mask_row(h, 0, i), pltpu.roll(x[h], LEVELS - 1, 0) - x[h], 0.0)
                    total = (flux_w[h] - flux[h]) + (below[2 * t + h] - above[2 * t + h])
                    total += vertical_coef * (up - pltpu.roll(up, 1, 0))
                    put(i, t, h, x[h], total)
            if put_seam is not None:
                turned = pltpu.roll(seam, 112, 1)
                upper = jnp.where(sub < 7, pltpu.roll(seam, 7, 0), pltpu.roll(turned, 7, 0))
                up = jnp.where(level_s + 1.0 < mask_row(2, 0, i), upper - seam, 0.0)
                turned = pltpu.roll(up, 16, 1)
                down = jnp.where(sub > 0, pltpu.roll(up, 1, 0), pltpu.roll(turned, 1, 0))
                total = (pltpu.roll(flux_s, 1, 1) - flux_s) + (below[4] - above[4]) + vertical_coef * (up - down)
                put_seam(i, seam, total)
            return above

        lax.fori_loop(first, last, step, north_flux(ref, seams, first - 1))

    def put_middle(i, t, h, x, total):
        M[i, h, 32 * t : 32 * t + 32, :] = x + time_step * total

    def put_middle_seam(i, x, total):
        Ms[i] = x + time_step * total

    laplace(X, Xs, 1, 23)
    tendency(X, Xs, 2, 22, put_middle, put_middle_seam)

    def put_updated(i, t, h, m, total):
        value = 0.5 * (at(X, i, h, t) + m) + 0.5 * time_step * total
        tout[h, pl.ds(512 * t + i - HALO, 32, stride=ROWS), :] = value
        part = jnp.where(level < mask_row(h, 0, i), value, 0.0)
        part = (part[0:8] + part[8:16]) + (part[16:24] + part[24:32])
        if t == 0:
            FS[i - HALO, h] = part
        else:
            FS[i - HALO, h] = FS[i - HALO, h] - 0.5 * part

    laplace(M, Ms, 3, 21)
    tendency(M, Ms, 4, 20, put_updated, None)

    stores = [
        pltpu.make_async_copy(tout.at[h], upd.at[:, pl.ds(128 * h, 128)], out_sem.at[h]) for h in range(2)
    ]
    for store in stores:
        store.start()

    for h in range(2):
        for tile in range(2):
            FO[h, tile] = jnp.sum(FS[8 * tile : 8 * tile + 8, h], axis=1) * (1.0 / math.sqrt(LEVELS))
    c_forcing = [
        send(FO.at[:, 1], gs, 0, (north, lo), s2, r2),
        send(FO.at[:, 0], gn, 1, (south, lo), s2, r2),
        send(FO.at[1], gw, 2, (la, east), s2, r2),
        send(FO.at[0], ge, 3, (la, west), s2, r2),
        send(FO.at[1, 1], gc.at[0], 4, (north, east), s2, r2),
        send(FO.at[1, 0], gc.at[1], 5, (south, east), s2, r2),
        send(FO.at[0, 1], gc.at[2], 6, (north, west), s2, r2),
        send(FO.at[0, 0], gc.at[3], 7, (south, west), s2, r2),
    ]
    surface = [p > 0.0 for p in depth]
    inverse = [jnp.where(surface[k], 1.0 / diagonal[k], 0.0) for k in range(3)]
    own_row = row < 16
    weight = [jnp.where(own_row, diagonal[k], 0.0) for k in range(2)]
    for copy in c_forcing:
        copy.wait()
    forcing = flat(
        [[FO[h, tile] for tile in range(2)] for h in range(2)],
        [gn[h] for h in range(2)], [gs[h] for h in range(2)],
        [ge[tile] for tile in range(2)], [gw[tile] for tile in range(2)],
        gc[3], gc[2], gc[1], gc[0],
    )

    def apply_b(parts):
        columns = [to_north(p) + to_south(p) for p in parts]
        mixed = [p + 0.5 * c for p, c in zip(parts, columns)]
        e, w = to_east(mixed), to_west(mixed)
        return [inverse[k] * (columns[k] + e[k] + w[k]) for k in range(3)]

    basis = [[forcing[k] * inverse[k] for k in range(3)]]
    basis.append(apply_b(basis[0]))
    for j in range(2, ITERS + 1):
        image = apply_b(basis[j - 1])
        basis.append([2.0 * image[k] - basis[j - 2][k] for k in range(3)])

    def partial(left, right):
        total = left[0] * right[0] + left[1] * right[1]
        total = total[0:8] + total[8:16]
        return jnp.sum(total, axis=0, keepdims=True)

    rows = []
    for j in range(ITERS):
        weighted = [weight[k] * basis[j][k] for k in range(2)]
        rows.append(partial(weighted, basis[j]))
        rows.append(partial(weighted, basis[j + 1]))
    sa[...] = jnp.concatenate(rows, axis=0)

    def gather(src, dst, me, size, partner, ss, rr):
        copies = []
        for k in range(1, size):
            copy = pltpu.make_async_remote_copy(
                src_ref=src, dst_ref=dst.at[me], send_sem=ss.at[k], recv_sem=rr.at[me],
                device_id=partner(k), device_id_type=MESH,
            )
            copy.start()
            copies.append(copy)
        dst[me] = src[...]
        for k in range(1, size):
            copies[k - 1].wait_send()
            other = lax.rem(me + k, size)
            pltpu.make_async_remote_copy(
                src_ref=src, dst_ref=dst.at[other], send_sem=ss.at[k], recv_sem=rr.at[other],
                device_id=partner(k), device_id_type=MESH,
            ).wait_recv()
        parts = [dst[k] for k in range(size)]
        while len(parts) > 1:
            parts = [parts[k] + parts[k + 1] for k in range(0, len(parts) - 1, 2)] + parts[len(parts) - len(parts) % 2 :]
        return parts[0]

    sb[...] = gather(sa, ra, me_a, size_a, partner_a, sas, sar)
    total = gather(sb, rb, me_b, size_b, partner_b, sbs, sbr)
    total = jnp.broadcast_to(jnp.sum(total, axis=1, keepdims=True), (8, 128))
    inner = [total[k : k + 1, :] for k in range(8)]
    c = inner[:2] + [2.0 * inner[k] - inner[k % 2] for k in range(2, 8)]

    def gram(i, j):
        return 0.5 * (c[i + j] + c[abs(i - j)])

    def ratio(top, bottom):
        good = jnp.logical_and(bottom > 0.0, top > 0.0)
        return jnp.where(good, top / jnp.where(good, bottom, 1.0), 0.0)

    zero = jnp.zeros_like(c[0])
    resid = [jnp.ones_like(zero)]
    direction = list(resid)
    pressure = [zero] * ITERS
    product = c[0]
    for k in range(ITERS):
        image = list(direction) + [zero]
        for j, value in enumerate(direction):
            if j == 0:
                image[1] = image[1] - value
            else:
                image[j + 1] = image[j + 1] - 0.5 * value
                image[j - 1] = image[j - 1] - 0.5 * value
        bottom = zero
        for i, value in enumerate(direction):
            line = zero
            for j, other in enumerate(image):
                line = line + other * gram(i, j)
            bottom = bottom + value * line
        alpha = ratio(product, bottom)
        for j, value in enumerate(direction):
            pressure[j] = pressure[j] + alpha * value
        if k + 1 < ITERS:
            resid = [a - alpha * b for a, b in zip(resid + [zero], image)]
            following = zero
            for i, value in enumerate(resid):
                line = zero
                for j, other in enumerate(resid):
                    line = line + other * gram(i, j)
                following = following + value * line
            beta = ratio(following, product)
            direction = [a + beta * b for a, b in zip(resid, direction + [zero])]
            product = following

    field = []
    for k in range(3):
        value = pressure[0] * basis[0][k]
        for j in range(1, ITERS):
            value = value + pressure[j] * basis[j][k]
        field.append(value)
    field_e = to_east(field)
    wet = [jnp.where(surface[k], 1.0, 0.0) for k in range(3)]
    wet_e = to_east(wet)
    for h in range(2):
        slope_e = wet[h] * wet_e[h] * (field_e[h] - field[h])
        slope_n = wet[h] * to_north(wet[h]) * (to_north(field[h]) - field[h])
        grad[0, :, 128 * h : 128 * h + 128] = slope_e[0:16]
        grad[1, :, 128 * h : 128 * h + 128] = slope_n[0:16]
    for store in stores:
        store.wait()


def body(lats, lons, tracers, east_velocity, north_velocity, column_levels, surface_term):
    tall = 2 * LEVELS * ROWS
    cells = tracers.reshape(tall, 256)
    east = east_velocity.reshape(LEVELS * ROWS, 256)
    north = north_velocity.reshape(LEVELS * ROWS, 256)
    size_a, size_b = lats // NZ, NZ * lons
    vmem = pltpu.VMEM
    scratch = [
        vmem((2, tall, 128), F32),
        vmem((2, 2, LEVELS * ROWS, 128), BF16),
        vmem((2, 2, LEVELS * ROWS, 128), F32),
        vmem((ROWS, 256), jnp.int32),
        vmem((ROWS, 256), F32),
        vmem((HIGH, 2, 64, 128), F32),
        vmem((HIGH, 2, 64, 128), F32),
        vmem((HIGH, 2, 64, 128), F32),
        vmem((HIGH, 2, 2, LEVELS, 128), F32),
        vmem((HIGH, 8, 128), F32),
        vmem((HIGH, 8, 128), F32),
        vmem((HIGH, 8, 128), F32),
        vmem((HIGH, 8, 128), F32),
        vmem((HIGH, 8, 128), F32),
        vmem((ROWS, 8, 128), F32),
        vmem((ROWS, 8, 128), F32),
        vmem((2, 4, 2, 8, 128), F32),
        vmem((2, 4, 2, 8, 128), F32),
        vmem((4, 2, 8, 128), F32),
        vmem((2, 2, 2, 64, 128), BF16),
        vmem((2, 2, 2, 64, 128), BF16),
        vmem((3, 2, 2, LEVELS, 128), BF16),
        vmem((2, 2, 2, LEVELS, 128), BF16),
        vmem((3, 2, 2, LEVELS, 128), BF16),
        vmem((2, 2, 2, LEVELS, 128), BF16),
        vmem((2, 2, 2, 8, 128), F32),
        vmem((2, 2, 8, 128), F32),
        vmem((2, 2, 8, 128), F32),
        vmem((2, 2, 8, 128), F32),
        vmem((2, 2, 8, 128), F32),
        vmem((4, 2, 8, 128), F32),
        vmem((2, 2, 8, 128), F32),
        vmem((2, 8, 128), F32),
        vmem((2, 8, 128), F32),
        vmem((2, 8, 128), F32),
        vmem((2, 8, 128), F32),
        vmem((4, 8, 128), F32),
        vmem((3, 5, HIGH, 128), F32),
        vmem((ROWS, 2, 8, 128), F32),
        vmem((2, tall, 128), F32),
        vmem((8, 128), F32),
        vmem((size_a, 8, 128), F32),
        vmem((8, 128), F32),
        vmem((size_b, 8, 128), F32),
        pltpu.SemaphoreType.DMA((8,)),
        pltpu.SemaphoreType.DMA((2,)),
        pltpu.SemaphoreType.DMA((21,)),
        pltpu.SemaphoreType.DMA((21,)),
        pltpu.SemaphoreType.DMA((8,)),
        pltpu.SemaphoreType.DMA((8,)),
        pltpu.SemaphoreType.DMA((size_a,)),
        pltpu.SemaphoreType.DMA((size_a,)),
        pltpu.SemaphoreType.DMA((size_b,)),
        pltpu.SemaphoreType.DMA((size_b,)),
    ]
    hbm = pl.BlockSpec(memory_space=pl.ANY)
    updated, gradient = pl.pallas_call(
        functools.partial(kernel, lats, lons),
        out_shape=(jax.ShapeDtypeStruct((tall, 256), F32), jax.ShapeDtypeStruct((2, ROWS, 256), F32)),
        in_specs=[hbm] * 5,
        out_specs=(hbm, pl.BlockSpec(memory_space=pltpu.VMEM)),
        scratch_shapes=scratch,
        compiler_params=pltpu.CompilerParams(
            collective_id=0, has_side_effects=True, vmem_limit_bytes=48 * 1024 * 1024
        ),
    )(cells, east, north, column_levels, surface_term)
    return updated.reshape(2, LEVELS, ROWS, 256), gradient


def solution(mesh):
    in_specs = (
        P(None, None, "lat", "lon"),
        P(None, "lat", "lon"),
        P(None, "lat", "lon"),
        P("lat", "lon"),
        P("lat", "lon"),
    )
    out_specs = (P(None, None, "lat", "lon"), P(None, "lat", "lon"))
    step = functools.partial(body, mesh.shape["lat"], mesh.shape["lon"])
    return jax.shard_map(step, mesh=mesh, in_specs=in_specs, out_specs=out_specs, check_vma=False)
```

time: 734 us -> 61.5 us (0.08); the launches traced: 724 us -> 61.2 us
  blocking collectives: 539 us -> 0 us
  starting transfers between devices: 73.9 us -> 0 us
  Pallas kernels: 0 us -> 54.5 us
  other arithmetic: 36 us -> 0 us
  waiting for transfers between devices: 33.8 us -> 0 us
  local copies, waits for them, and re-layouts: 30.2 us -> 6.14 us
  between operations: 10.6 us -> 0.65 us
    psum x7 -> x0, blocking collectives: 539 us -> none  [totals(): return lax.psum(local, ('lat', 'lon'))]
    ppermute x32 -> x0, starting transfers between devices: 73.9 us -> none  [the longest x16 53.9 us: extended(): lax.ppermute(head, axis, [((i + 1) % count, i) for i in range(count)])]
    pallas_call x0 -> x1, Pallas kernels: none -> 54.5 us  [body(): pl.pallas_call(functools.partial(kernel, lats, lons), out_shape=(jax.Shap...]
    ppermute x32 -> x0, waiting for transfers between devices: 33.8 us -> none  [the longest x16 17.7 us: extended(): lax.ppermute(head, axis, [((i + 1) % count, i) for i in range(count)])]
    slice x23 -> x0, local copies, waits for them, and re-layouts: 17.5 us -> none  [the longest x17 8.41 us: extended(): lax.slice_in_dim(cells, cells.shape[dim] - width, cells.shape[dim], axis=...]
    mul x3 -> x0, other arithmetic: 9.91 us -> none  [the longest x2 6.56 us: laplace_pad(): return masks[0] * total]
    ppermute x4 -> x0, local copies, waits for them, and re-layouts: 8.17 us -> none  [the longest x2 4.09 us: extended(): lax.ppermute(tail, axis, [(i, (i + 1) % count) for i in range(count)])]
    select_n x8 -> x0, other arithmetic: 7.85 us -> none  [fix_rims(): jnp.where(cut.reshape(shape_list), jnp.zeros((), padded.dtype), padded)]
  transfers between devices with their start and end apart: 32 -> 0, of which waited for: 20 -> 0; matrix products, arithmetic and copies ran while one was open for 3% -> 0% of each run, Pallas kernels for 0% -> 0%
where the time goes in v1:
time: 61.5 us; the launch traced here: 61.2 us
  Pallas kernels  54.5 us (89%)
  local copies, waits for them, and re-layouts  6.14 us (10%)
  between operations  0.65 us (1%)
    pallas_call x1, Pallas kernels, body(): pl.pallas_call(functools.partial(kernel, lats, lons), out_shape=(jax.Shap...  54.5 us
    unnamed x12, local copies, waits for them, and re-layouts  6.14 us

profile of v1, /device:TPU:1, one launch (start us, length us, event | category | flops | bytes accessed | tf_op | source)
XLA Modules:
  0.0 61.2 jit_solution(5366172197798110981)
XLA Ops:
  0.6 0.0 copy-start
  0.6 1.2 %copy-done = f32[2,32,16,256]{3,2,1,0:T(8,128)S(1)} copy-done((f32[2,32,16,256]{3,2,1,0:T(8,128)S(1)}, f32[2,32,16,256]{3,2,1,0:T(8,128)}, u32[]{:S(2)}) %copy-start) | copy-done | bytes 1048600
  1.9 0.0 copy-start.1
  1.9 0.9 %copy-done.1 = bf16[32,16,256]{2,1,0:T(8,128)(2,1)S(1)} copy-done((bf16[32,16,256]{2,1,0:T(8,128)(2,1)S(1)}, bf16[32,16,256]{2,1,0:T(8,128)(2,1)}, u32[]{:S(2)}) %copy-start.1) | copy-done | bytes 262168
  2.8 0.0 copy-start.2
  2.8 0.9 %copy-done.2 = bf16[32,16,256]{2,1,0:T(8,128)(2,1)S(1)} copy-done((bf16[32,16,256]{2,1,0:T(8,128)(2,1)S(1)}, bf16[32,16,256]{2,1,0:T(8,128)(2,1)}, u32[]{:S(2)}) %copy-start.2) | copy-done | bytes 262168
  3.8 0.0 copy-start.3
  3.8 0.7 %copy-done.3 = s32[16,256]{1,0:T(8,128)S(1)} copy-done((s32[16,256]{1,0:T(8,128)S(1)}, s32[16,256]{1,0:T(8,128)}, u32[]{:S(2)}) %copy-start.3) | copy-done | bytes 16408
  4.5 0.0 copy-start.4
  4.5 0.7 %copy-done.4 = f32[16,256]{1,0:T(8,128)S(1)} copy-done((f32[16,256]{1,0:T(8,128)S(1)}, f32[16,256]{1,0:T(8,128)}, u32[]{:S(2)}) %copy-start.4) | copy-done | bytes 16408
  5.2 54.5 %shard_map.68 = (f32[1024,256]{1,0:T(8,128)S(1)}, f32[2,16,256]{2,1,0:T(8,128)S(1)}) custom-call(f32[1024,256]{1,0:T(8,128)S(1)} %bitcast.4, bf16[512,256]{1,0:T(8,128)(2,1)S(1)} %bitcast.6, bf16[512,256]{1,0:T(8,128)(2,1)S(1)} %bitcast.7, s32[16,256]{1,0:T(8,128)S(1)} %copy-done.3, f32[16,256]{1,0:T(8,128)S(1)} %copy-done.4), custom_call_target="tpu_custom_call" | custom-call | tf_op jit(solution)/shard_map/pallas_call | solution.py:605
  59.7 1.0 %copy.9 = f32[2,32,16,256]{3,2,1,0:T(8,128)} copy(f32[2,32,16,256]{3,2,1,0:T(8,128)S(1)} %bitcast.5) | data formatting | bytes 2097152
  60.6 0.6 %copy.10 = f32[2,16,256]{2,1,0:T(8,128)} copy(f32[2,16,256]{2,1,0:T(8,128)S(1)} %get-tuple-element.9) | data formatting | bytes 65536
Async XLA Ops:
  0.6 1.2 %copy-start = (f32[2,32,16,256]{3,2,1,0:T(8,128)S(1)}, f32[2,32,16,256]{3,2,1,0:T(8,128)}, u32[]{:S(2)}) copy-start(f32[2,32,16,256]{3,2,1,0:T(8,128)} %param.5) | copy-start | bytes 3145732
  1.9 0.9 %copy-start.1 = (bf16[32,16,256]{2,1,0:T(8,128)(2,1)S(1)}, bf16[32,16,256]{2,1,0:T(8,128)(2,1)}, u32[]{:S(2)}) copy-start(bf16[32,16,256]{2,1,0:T(8,128)(2,1)} %param.6) | copy-start | bytes 786436
  2.8 0.9 %copy-start.2 = (bf16[32,16,256]{2,1,0:T(8,128)(2,1)S(1)}, bf16[32,16,256]{2,1,0:T(8,128)(2,1)}, u32[]{:S(2)}) copy-start(bf16[32,16,256]{2,1,0:T(8,128)(2,1)} %param.7) | copy-start | bytes 786436
  3.8 0.7 %copy-start.3 = (s32[16,256]{1,0:T(8,128)S(1)}, s32[16,256]{1,0:T(8,128)}, u32[]{:S(2)}) copy-start(s32[16,256]{1,0:T(8,128)} %levels_in.1) | copy-start | bytes 49156
  4.5 0.7 %copy-start.4 = (f32[16,256]{1,0:T(8,128)S(1)}, f32[16,256]{1,0:T(8,128)}, u32[]{:S(2)}) copy-start(f32[16,256]{1,0:T(8,128)} %term_in.1) | copy-start | bytes 49156

commit v2 on v1

v2 whole, which is shorter than its diff:
```python
import functools
import math

import jax
import jax.numpy as jnp
from jax import lax
from jax.experimental import pallas as pl
from jax.experimental.pallas import tpu as pltpu
from jax.sharding import PartitionSpec as P

MESH = pl.DeviceIdType.MESH
F32 = jnp.float32
BF16 = jnp.bfloat16

ITERS = 4
LEVELS = 32
ROWS = 16
HALO = 4
HIGH = ROWS + 2 * HALO
NX = 4
NZ = 2

time_step = 0.5
biharm_coef = 0.05
vertical_coef = 0.8


def iota(shape, axis):
    return lax.broadcasted_iota(jnp.int32, shape, axis)


def kernel(
    lats, lons, trc, vel_e, vel_n, levels_in, term_in, out, grad,
    vin, vf, levi, termi, X, M, LP, SX, V, U, Xs, Ms, Us, Vs, Qt, Qv, pack, pack_in, corner_in,
    xb, xb_in, vbn, vbs, vbn_in, vbs_in, FL, FT, ft_in,
    FO, gn, gs, ge, gw, gc, MK, FS, tout, sa, ra, sb, rb,
    in_sem, s1, r1, s2, r2, sas, sar, sbs, sbr,
):
    la, lo = lax.axis_index("lat"), lax.axis_index("lon")
    north, south = lax.rem(la + 1, lats), lax.rem(la + lats - 1, lats)
    east, west = lax.rem(lo + 1, lons), lax.rem(lo + lons - 1, lons)
    ny = lats // (NX * NZ)
    y, zx = la // (NX * NZ), lax.rem(la, NX * NZ)
    zz, xx = zx // NX, lax.rem(zx, NX)
    size_a, size_b = ny * NX, NZ * lons
    me_a, me_b = y * NX + xx, zz * lons + lo

    def partner_a(k):
        a = lax.rem(me_a + k, size_a)
        return ((a // NX) * NZ + zz) * NX + lax.rem(a, NX), lo

    def partner_b(k):
        b = lax.rem(me_b + k, size_b)
        return (y * NZ + b // lons) * NX + xx, lax.rem(b, lons)

    loads = [
        pltpu.make_async_copy(levels_in, levi, in_sem.at[0]),
        pltpu.make_async_copy(term_in, termi, in_sem.at[1]),
    ]
    edge_rows = [0, 1, 2, 3, 12, 13, 14, 15]
    inner_rows = list(range(4, 12))

    def load_rows(rows):
        return [
            pltpu.make_async_copy(
                trc.at[:, r, pl.ds(128 * h, 128)], X.at[r + HALO, h, pl.ds(8, 64)], in_sem.at[6 + 2 * r + h]
            )
            for r in rows
            for h in range(2)
        ]

    x_loads = load_rows(edge_rows)
    v_loads = [
        pltpu.make_async_copy(src.at[:, pl.ds(128 * h, 128)], vin.at[w, h], in_sem.at[2 + 2 * w + h])
        for w, src in enumerate((vel_e, vel_n))
        for h in range(2)
    ]
    y_loads = load_rows(inner_rows)
    for load in loads + x_loads + v_loads + y_loads:
        load.start()

    barrier = pltpu.get_barrier_semaphore()
    around = [
        (north, lo), (south, lo), (la, east), (la, west),
        (north, east), (south, east), (north, west), (south, west),
    ]
    partners = [partner_a(k) for k in range(1, size_a)] + [partner_b(k) for k in range(1, size_b)]
    for device in around + partners:
        pl.semaphore_signal(barrier, inc=1, device_id=device, device_id_type=MESH)

    def send(src, dst, k, device, ss=s1, rr=r1):
        copy = pltpu.make_async_remote_copy(
            src_ref=src, dst_ref=dst, send_sem=ss.at[k], recv_sem=rr.at[k], device_id=device, device_id_type=MESH
        )
        copy.start()
        return copy

    lane = iota((8, 128), 1)
    sub = iota((8, 128), 0)
    lane16 = lax.rem(lane, 16)
    laneq = lane // 16

    def row_pairs(first, last, step, carry=0):
        def pair(n, carry):
            return step(first + 2 * n + 1, step(first + 2 * n, carry))

        return lax.fori_loop(0, (last - first) // 2, pair, carry)

    for load in loads:
        load.wait()
    for h in range(2):
        for tile in range(2):
            FL[h, tile, 0] = levi[8 * tile : 8 * tile + 8, 128 * h : 128 * h + 128].astype(F32)
            FL[h, tile, 1] = termi[8 * tile : 8 * tile + 8, 128 * h : 128 * h + 128]

    for h in range(2):
        FT[0, h] = jnp.where(sub < 4, pltpu.roll(FL[h, 1, 0], 4, 0), FL[h, 1, 1])
        FT[1, h] = jnp.where(sub < 4, FL[h, 0, 0], pltpu.roll(FL[h, 0, 1], 4, 0))
    for side in range(2):
        packed = jnp.zeros((8, 128), F32)
        for f in range(2):
            for tile in range(2):
                j = 2 * f + tile
                turn = (4 * j + 4) % 128 if side == 0 else 4 * j
                value = FL[1 - side, tile, f]
                packed = jnp.where(lane // 4 == j, pltpu.roll(value, turn, 1) if turn else value, packed)
        pack[side, 0] = packed
        pack[side, 9] = packed

    for load in x_loads:
        load.wait()
    for j in range(3):
        xb[0, j] = X[16 + j, :, 8:72, :].astype(BF16)
        xb[1, j] = X[5 + j, :, 8:72, :].astype(BF16)

    for load in v_loads:
        load.wait()

    def widen(n, carry):
        rows = pl.ds(pl.multiple_of(64 * n, 64), 64)
        for w in range(2):
            for h in range(2):
                vf[w, h, rows, :] = vin[w, h, rows, :].astype(F32) * (0.5 * time_step)
        return carry

    lax.fori_loop(0, 8, widen, 0)

    def fill_v(i, carry):
        for w in range(2):
            for h in range(2):
                V[i, w, h] = vf[w, h, pl.ds(i - HALO, 32, stride=ROWS), :]
        return carry

    row_pairs(HALO, HALO + ROWS, fill_v)
    for j in range(3):
        vbn[j] = V[17 + j].astype(BF16)
    for j in range(2):
        vbs[j] = V[4 + j].astype(BF16)

    def seam_of(parts):
        out = jnp.zeros((8, 128), F32)
        for q, (low, high) in enumerate(parts):
            both = jnp.where(lane >= 124, high, low)
            out = jnp.where(laneq == q, pltpu.roll(both, (16 * q + 4) % 128, 1), out)
        return out

    def seam_x(i):
        return seam_of([(X[i, 0, 8 * q + 8 : 8 * q + 16, :], X[i, 1, 8 * q + 8 : 8 * q + 16, :]) for q in range(8)])

    def seam_v(i):
        return seam_of(
            [
                (V[i, q // 4, 0, 8 * (q % 4) : 8 * (q % 4) + 8, :], V[i, q // 4, 1, 8 * (q % 4) : 8 * (q % 4) + 8, :])
                for q in range(8)
            ]
        )

    def pack_rows(i, carry):
        Qt[i - HALO] = seam_x(i)
        Qv[i - HALO] = seam_v(i)
        return carry

    for load in y_loads:
        load.wait()
    row_pairs(HALO, HALO + ROWS, pack_rows)
    for a in range(4):
        for w, Q in enumerate((Qt, Qv)):
            for side in range(2):
                packed = jnp.zeros((8, 128), F32)
                for n in range(4):
                    turn = (4 * n - 4 * side) % 128
                    value = Q[4 * a + n]
                    packed = jnp.where(lane16 // 4 == n, pltpu.roll(value, turn, 1) if turn else value, packed)
                pack[side, 1 + 2 * a + w] = packed

    pl.semaphore_wait(barrier, len(around) + len(partners))

    body_rows = pl.ds(8, 64)
    c_side = [
        send(pack.at[0, pl.ds(0, 9)], pack_in.at[0], 0, (la, east)),
        send(pack.at[1, pl.ds(0, 9)], pack_in.at[1], 1, (la, west)),
    ]
    c_far = [
        send(pack.at[0, pl.ds(7, 3)], corner_in.at[0], 2, (north, east)),
        send(pack.at[0, pl.ds(0, 3)], corner_in.at[1], 3, (south, east)),
        send(pack.at[1, pl.ds(7, 3)], corner_in.at[2], 4, (north, west)),
        send(pack.at[1, pl.ds(0, 3)], corner_in.at[3], 5, (south, west)),
        send(FT.at[0], ft_in.at[0], 6, (north, lo)),
        send(FT.at[1], ft_in.at[1], 7, (south, lo)),
        send(X.at[19, :, body_rows], X.at[3, :, body_rows], 8, (north, lo)),
        send(X.at[4, :, body_rows], X.at[20, :, body_rows], 9, (south, lo)),
        send(xb.at[0], xb_in.at[0], 10, (north, lo)),
        send(xb.at[1], xb_in.at[1], 11, (south, lo)),
        send(vbn.at[pl.ds(1, 2)], vbn_in.at[pl.ds(1, 2)], 12, (north, lo)),
        send(vbn.at[0, 1], vbn_in.at[0, 1], 13, (north, lo)),
        send(vbs, vbs_in, 14, (south, lo)),
    ]

    def flat(own, n, s, e, w, ne, se, nw, sw):
        parts = [jnp.concatenate([own[h][0], own[h][1], jnp.where(sub < 4, n[h], s[h])], axis=0) for h in range(2)]
        right = jnp.concatenate([e[0], e[1], jnp.where(sub < 4, ne, se)], axis=0)
        left = jnp.concatenate([w[0], w[1], jnp.where(sub < 4, nw, sw)], axis=0)
        parts.append(jnp.where(iota((24, 128), 1) < 64, right, left))
        return parts

    def to_east(parts):
        rolled = [pltpu.roll(p, 127, 1) for p in parts]
        last = iota(parts[0].shape, 1) == 127
        return [jnp.where(last, rolled[(k + 1) % 3], rolled[k]) for k in range(3)]

    def to_west(parts):
        rolled = [pltpu.roll(p, 1, 1) for p in parts]
        first = iota(parts[0].shape, 1) == 0
        return [jnp.where(first, rolled[(k + 2) % 3], rolled[k]) for k in range(3)]

    def to_north(part):
        return pltpu.roll(part, 23, 0)

    def to_south(part):
        return pltpu.roll(part, 1, 0)

    def put_masks(depth):
        east_depth = to_east(depth)
        for h in range(2):
            MK[h, 0] = depth[h]
            MK[h, 1] = jnp.minimum(depth[h], east_depth[h])
            MK[h, 2] = jnp.minimum(depth[h], to_north(depth[h]))

    dry = jnp.zeros((8, 128), F32)
    put_masks([jnp.concatenate([FL[h, 0, 0], FL[h, 1, 0], dry], axis=0) for h in range(2)] + [jnp.zeros((24, 128), F32)])

    level = iota((LEVELS, 128), 0).astype(F32)
    lane_f = iota((LEVELS, 128), 1)
    mixing = time_step * biharm_coef
    lifting = time_step * vertical_coef
    places = [(t, h) for t in range(2) for h in range(2)]

    def mask_row(h, n, i):
        return MK[h, n, pl.ds(jnp.where(i >= HALO, i - HALO, i + 20), 1), :]

    def at(ref, i, h, t, up=0):
        return ref[i, h, 8 + 32 * t + up : 40 + 32 * t + up, :]

    def bare(ref, i, h, t):
        return ref[i, h, 32 * t : 32 * t + 32, :]

    def shift_e(halves):
        low, high = pltpu.roll(halves[0], 127, 1), pltpu.roll(halves[1], 127, 1)
        return [jnp.where(lane_f == 127, high, low), high]

    def shift_w(halves):
        low, high = pltpu.roll(halves[0], 1, 1), pltpu.roll(halves[1], 1, 1)
        return [low, jnp.where(lane_f == 0, low, high)]

    def north_step(ref, i):
        wet = [level < mask_row(h, 2, i) for h in range(2)]
        return [jnp.where(wet[h], at(ref, i + 1, h, t) - at(ref, i, h, t), 0.0) for t, h in places]

    def laplace(ref, first, last):
        def step(i, below):
            above = north_step(ref, i)
            wet = [level < mask_row(h, 1, i) for h in range(2)]
            for t in range(2):
                x = [at(ref, i, h, t) for h in range(2)]
                xe = shift_e(x)
                flux = []
                for h in range(2):
                    SX[i, h, 32 * t : 32 * t + 32, :] = x[h] + xe[h]
                    flux.append(jnp.where(wet[h], xe[h] - x[h], 0.0))
                flux_w = shift_w(flux)
                for h in range(2):
                    total = (flux[h] - flux_w[h]) + (above[2 * t + h] - below[2 * t + h])
                    LP[i, h, 32 * t : 32 * t + 32, :] = mixing * total
            return above

        row_pairs(first, last, step, north_step(ref, first - 1))

    def north_flux(ref, i):
        flux = []
        wet = [level < mask_row(h, 2, i) for h in range(2)]
        for t, h in places:
            value = V[i, 1, h] * (at(ref, i, h, t) + at(ref, i + 1, h, t))
            value += bare(LP, i + 1, h, t) - bare(LP, i, h, t)
            flux.append(jnp.where(wet[h], value, 0.0))
        return flux

    def tendency(ref, first, last, put):
        def step(i, below):
            above = north_flux(ref, i)
            wet_e = [level < mask_row(h, 1, i) for h in range(2)]
            deep = [mask_row(h, 0, i) for h in range(2)]
            wet_u = [level + 1.0 < deep[h] for h in range(2)]
            wet_d = [jnp.logical_and(level > 0.0, level < deep[h]) for h in range(2)]
            results = []
            for t in range(2):
                lap = [bare(LP, i, h, t) for h in range(2)]
                lape = shift_e(lap)
                flux = []
                for h in range(2):
                    value = V[i, 0, h] * bare(SX, i, h, t) + (lape[h] - lap[h])
                    flux.append(jnp.where(wet_e[h], value, 0.0))
                flux_w = shift_w(flux)
                for h in range(2):
                    x = at(ref, i, h, t)
                    up = jnp.where(wet_u[h], at(ref, i, h, t, 1) - x, 0.0)
                    down = jnp.where(wet_d[h], x - at(ref, i, h, t, -1), 0.0)
                    total = (flux_w[h] - flux[h]) + (below[2 * t + h] - above[2 * t + h])
                    results.append((x, total + lifting * (up - down)))
            put(i, results)
            return above

        row_pairs(first, last, step, north_flux(ref, first - 1))

    def put_middle(i, results):
        for (t, h), (x, half) in zip(places, results):
            M[i, h, 8 + 32 * t : 40 + 32 * t, :] = x + half

    def rim(value):
        return jnp.where(lane16 < 4, value, pltpu.roll(value, 120, 1))

    def patched(value, rims, q, h):
        pulled = pltpu.roll(rims, (124 - 16 * q) % 128, 1)
        return jnp.where(lane < 2, pulled, value) if h == 0 else jnp.where(lane >= 126, pulled, value)

    def patch_middle(i, carry):
        value = Ms[i]
        rims = rim(value)
        parts = []
        for q in range(8):
            pair = [patched(M[i, h, 8 * q + 8 : 8 * q + 16, :], rims, q, h) for h in range(2)]
            for h in range(2):
                M[i, h, 8 * q + 8 : 8 * q + 16, :] = pair[h]
            parts.append(tuple(pair))
        own = seam_of(parts)
        own = jnp.where(lane16 < 4, own, pltpu.roll(own, 8, 1))
        Ms[i] = jnp.where(jnp.logical_and(lane16 >= 4, lane16 < 12), value, own)
        return carry

    def put_updated(i, results):
        rims = rim(Xs[i])
        wet = [level < mask_row(h, 0, i) for h in range(2)]
        sums = [[], []]
        for (t, h), (m, half) in zip(places, results):
            value = 0.5 * ((at(X, i, h, t) + m) + half)
            value = jnp.concatenate(
                [patched(value[8 * g : 8 * g + 8], rims, 4 * t + g, h) for g in range(4)], axis=0
            )
            U[i - HALO, h, 32 * t : 32 * t + 32, :] = value
            part = jnp.where(wet[h], value, 0.0)
            sums[t].append((part[0:8] + part[8:16]) + (part[16:24] + part[24:32]))
        for h in range(2):
            FS[i - HALO, h] = sums[0][h] - 0.5 * sums[1][h]

    def seam_row(own, from_east, from_west, n):
        value = jnp.where(lane16 < 4, own, pltpu.roll(own, 8, 1))
        right = pltpu.roll(from_east, (4 - 4 * n) % 128, 1) if n != 1 else from_east
        left = pltpu.roll(from_west, (8 - 4 * n) % 128, 1) if n != 2 else from_west
        value = jnp.where(lane16 // 4 == 1, right, value)
        return jnp.where(lane16 // 4 == 2, left, value)

    def put_velocity(i, both):
        other = pltpu.roll(both, 64, 1)
        Us[i] = jnp.where(lane < 64, both, other)
        Vs[i] = jnp.where(lane < 64, other, both)

    level_s = (sub + 8 * lax.rem(laneq, 4)).astype(F32)

    def seam_masks(depth, rows):
        wide = iota(depth[0].shape, 1)
        seam_e = jnp.where(wide >= 124, depth[1], depth[2])
        seam_w = jnp.where(wide >= 124, depth[2], depth[0])
        base = jnp.where(wide < 8, pltpu.roll(seam_e, 4, 1), pltpu.roll(seam_w, 12, 1))
        base = jnp.where(wide < 16, base, 0.0)
        for turn in (16, 32, 64):
            base = base + pltpu.roll(base, turn, 1)
        deep = jnp.stack([jnp.broadcast_to(base[r : r + 1, :], (8, 128)) for r in rows], axis=0)
        wet_e = level_s[None] < jnp.minimum(deep, pltpu.roll(deep, 127, 2))
        wet_n = level_s[None] < jnp.minimum(deep[:-1], deep[1:])
        return wet_e, wet_n, level_s[None] + 1.0 < deep

    def seam_tendency(ref, first, last, masks):
        wet_e, wet_n, wet_u = masks
        x = ref[first - 2 : last + 2]
        xe = pltpu.roll(x, 127, 2)
        flux = jnp.where(wet_e, xe - x, 0.0)
        flux_n = jnp.where(wet_n, x[1:] - x[:-1], 0.0)
        lap = mixing * ((flux - pltpu.roll(flux, 1, 2))[1:-1] + (flux_n[1:] - flux_n[:-1]))
        x, xe = x[1:-1], xe[1:-1]
        flux = Us[first:last] * (x + xe)[1:-1] + (pltpu.roll(lap, 127, 2) - lap)[1:-1]
        flux = jnp.where(wet_e[2:-2], flux, 0.0)
        flux_n = Vs[first - 1 : last] * (x[1:] + x[:-1]) + (lap[1:] - lap[:-1])
        flux_n = jnp.where(wet_n[1:-1], flux_n, 0.0)
        x = x[1:-1]
        turned = pltpu.roll(x, 112, 2)
        upper = jnp.where(sub[None] < 7, pltpu.roll(x, 7, 1), pltpu.roll(turned, 7, 1))
        up = jnp.where(wet_u[2:-2], upper - x, 0.0)
        turned = pltpu.roll(up, 16, 2)
        down = jnp.where(sub[None] > 0, pltpu.roll(up, 1, 1), pltpu.roll(turned, 1, 1))
        total = (pltpu.roll(flux, 1, 2) - flux) + (flux_n[:-1] - flux_n[1:])
        return x, total + lifting * (up - down)

    def part_of(masks, first, last):
        return masks[0][first:last], masks[1][first : last - 1], masks[2][first:last]

    def seam_middle(first, last, masks):
        x, half = seam_tendency(Xs, first, last, masks)
        Ms[first:last] = x + half

    def seam_updated(first, last, masks):
        m, half = seam_tendency(Ms, first, last, masks)
        Xs[first:last] = 0.5 * ((Xs[first:last] + m) + half)

    laplace(X, 5, 19)
    tendency(X, 6, 18, put_middle)

    for copy in c_side:
        copy.wait()
    for a in range(4):
        for n in range(4):
            i = HALO + 4 * a + n
            Xs[i] = seam_row(Qt[4 * a + n], pack_in[1, 1 + 2 * a], pack_in[0, 1 + 2 * a], n)
            put_velocity(i, seam_row(Qv[4 * a + n], pack_in[1, 2 + 2 * a], pack_in[0, 2 + 2 * a], n))

    def beside(f, tile, right, left):
        j = 2 * f + tile
        right = pltpu.roll(right, 128 - 4 * j, 1) if j else right
        return jnp.where(lane < 64, right, pltpu.roll(left, 124 - 4 * j, 1))

    inside = [[jnp.concatenate([FL[h, tile, f] for tile in range(2)], axis=0) for h in range(2)] for f in range(2)]
    for f in range(2):
        inside[f].append(jnp.concatenate([beside(f, tile, pack_in[1, 0], pack_in[0, 0]) for tile in range(2)], axis=0))
    masks = seam_masks(inside[0], range(16))
    seam_middle(6, 18, masks)
    row_pairs(6, 18, patch_middle)
    seam_updated(8, 16, part_of(masks, 2, 14))
    laplace(M, 7, 17)
    tendency(M, 8, 16, put_updated)

    for copy in c_far:
        copy.wait()
    for j in range(3):
        X[j, :, 8:72, :] = xb_in[0, j].astype(F32)
        X[21 + j, :, 8:72, :] = xb_in[1, j].astype(F32)
    for j in range(2):
        V[2 + j] = vbn_in[1 + j].astype(F32)
        V[20 + j] = vbs_in[j].astype(F32)
    V[1, 1] = vbn_in[0, 1].astype(F32)

    rims = []
    for f in range(2):
        rim_f = []
        for h in range(2):
            from_north, from_south = ft_in[1, h], ft_in[0, h]
            if f == 0:
                rim_f.append(jnp.where(sub < 4, from_north, pltpu.roll(from_south, 4, 0)))
            else:
                rim_f.append(jnp.where(sub < 4, pltpu.roll(from_north, 4, 0), from_south))
        above = beside(f, 0, corner_in[3, 0], corner_in[1, 0])
        below = beside(f, 1, corner_in[2, 2], corner_in[0, 2])
        rim_f.append(jnp.where(sub < 4, above, below))
        rims.append(rim_f)
    no_north = (sub < 4).astype(jnp.int32) * (la == lats - 1).astype(jnp.int32)
    no_south = (sub >= 4).astype(jnp.int32) * (la == 0).astype(jnp.int32)
    outside = (no_north + no_south) > 0
    rims[0] = [jnp.where(outside, 0.0, p) for p in rims[0]]
    depth = [jnp.concatenate([inside[0][k], rims[0][k]], axis=0) for k in range(3)]
    diagonal = [6.0 + jnp.concatenate([inside[1][k], rims[1][k]], axis=0) for k in range(3)]
    put_masks(depth)

    for first in (1, 19):
        laplace(X, first, first + 4)
    for first in (2, 18):
        tendency(X, first, first + 4, put_middle)
    for n in range(4):
        Xs[n] = seam_row(seam_x(n), corner_in[2, 0], corner_in[0, 0], n)
        Xs[20 + n] = seam_row(seam_x(20 + n), corner_in[3, 1], corner_in[1, 1], n)
        if n > 0:
            put_velocity(n, seam_row(seam_v(n), corner_in[2, 1], corner_in[0, 1], n))
        if n < 2:
            put_velocity(20 + n, seam_row(seam_v(20 + n), corner_in[3, 2], corner_in[1, 2], n))
    masks_low = seam_masks(depth, list(range(20, 24)) + list(range(6)))
    masks_high = seam_masks(depth, range(10, 20))
    seam_middle(2, 6, part_of(masks_low, 0, 8))
    seam_middle(18, 22, part_of(masks_high, 2, 10))
    row_pairs(2, 6, patch_middle)
    row_pairs(18, 22, patch_middle)
    seam_updated(4, 8, part_of(masks_low, 2, 10))
    seam_updated(16, 20, part_of(masks_high, 0, 8))
    laplace(M, 3, 7)
    laplace(M, 17, 21)
    tendency(M, 4, 8, put_updated)
    tendency(M, 16, 20, put_updated)

    def forcing_rows(first, last, h):
        return jnp.sum(FS[first:last, h], axis=1) * (1.0 / math.sqrt(LEVELS))

    for h in range(2):
        for tile in range(2):
            FO[h, tile] = forcing_rows(8 * tile, 8 * tile + 8, h)
    c_forcing = [
        send(FO.at[1, 1], gc.at[0], 4, (north, east), s2, r2),
        send(FO.at[1, 0], gc.at[1], 5, (south, east), s2, r2),
        send(FO.at[0, 1], gc.at[2], 6, (north, west), s2, r2),
        send(FO.at[0, 0], gc.at[3], 7, (south, west), s2, r2),
        send(FO.at[:, 1], gs, 0, (north, lo), s2, r2),
        send(FO.at[:, 0], gn, 1, (south, lo), s2, r2),
    ]
    c_forcing += [
        send(FO.at[1], gw, 2, (la, east), s2, r2),
        send(FO.at[0], ge, 3, (la, west), s2, r2),
    ]


    def put_rows(i, carry):
        for h in range(2):
            tout[h, pl.ds(i, 64, stride=ROWS), :] = U[i, h]
        return carry

    def put_out(n, carry):
        rows = pl.ds(pl.multiple_of(128 * n, 128), 128)
        for h in range(2):
            out[rows, 128 * h : 128 * h + 128] = tout[h, rows, :]
        return carry

    row_pairs(0, ROWS, put_rows)
    lax.fori_loop(0, 8, put_out, 0)
    row = iota((24, 128), 0)
    surface = [p > 0.0 for p in depth]
    inverse = [jnp.where(surface[k], 1.0 / diagonal[k], 0.0) for k in range(3)]
    weight = [jnp.where(row < 16, diagonal[k], 0.0) for k in range(2)]
    for copy in c_forcing:
        copy.wait()
    forcing = flat(
        [[FO[h, tile] for tile in range(2)] for h in range(2)],
        [gn[h] for h in range(2)], [gs[h] for h in range(2)],
        [ge[tile] for tile in range(2)], [gw[tile] for tile in range(2)],
        gc[3], gc[2], gc[1], gc[0],
    )

    def apply_b(parts):
        columns = [to_north(p) + to_south(p) for p in parts]
        mixed = [p + 0.5 * c for p, c in zip(parts, columns)]
        e, w = to_east(mixed), to_west(mixed)
        return [inverse[k] * (columns[k] + e[k] + w[k]) for k in range(3)]

    basis = [[forcing[k] * inverse[k] for k in range(3)]]
    basis.append(apply_b(basis[0]))
    for j in range(2, ITERS + 1):
        image = apply_b(basis[j - 1])
        basis.append([2.0 * image[k] - basis[j - 2][k] for k in range(3)])

    def partial(left, right):
        total = left[0] * right[0] + left[1] * right[1]
        total = total[0:8] + total[8:16]
        return jnp.sum(total, axis=0, keepdims=True)

    rows = []
    for j in range(ITERS):
        weighted = [weight[k] * basis[j][k] for k in range(2)]
        rows.append(partial(weighted, basis[j]))
        rows.append(partial(weighted, basis[j + 1]))
    sums = jnp.sum(jnp.concatenate(rows, axis=0), axis=1, keepdims=True)
    sa[...] = jnp.sum(jnp.where(lane == sub, sums, 0.0), axis=0, keepdims=True)

    def gather(src, dst, me, size, partner, ss, rr):
        copies = []
        for k in range(1, size):
            copy = pltpu.make_async_remote_copy(
                src_ref=src, dst_ref=dst.at[me], send_sem=ss.at[k], recv_sem=rr.at[me],
                device_id=partner(k), device_id_type=MESH,
            )
            copy.start()
            copies.append(copy)
        dst[me] = src[...]
        for k in range(1, size):
            copies[k - 1].wait_send()
            other = lax.rem(me + k, size)
            pltpu.make_async_remote_copy(
                src_ref=src, dst_ref=dst.at[other], send_sem=ss.at[k], recv_sem=rr.at[other],
                device_id=partner(k), device_id_type=MESH,
            ).wait_recv()
        parts = [dst[k] for k in range(size)]
        while len(parts) > 1:
            parts = [parts[k] + parts[k + 1] for k in range(0, len(parts) - 1, 2)] + parts[len(parts) - len(parts) % 2 :]
        return parts[0]

    sb[...] = gather(sa, ra, me_a, size_a, partner_a, sas, sar)
    total = gather(sb, rb, me_b, size_b, partner_b, sbs, sbr)
    inner = [jnp.broadcast_to(total[:, k : k + 1], (1, 128)) for k in range(8)]
    c = inner[:2] + [2.0 * inner[k] - inner[k % 2] for k in range(2, 8)]

    def gram(i, j):
        return 0.5 * (c[i + j] + c[abs(i - j)])

    def ratio(top, bottom):
        good = jnp.logical_and(bottom > 0.0, top > 0.0)
        return jnp.where(good, top / jnp.where(good, bottom, 1.0), 0.0)

    zero = jnp.zeros_like(c[0])
    resid = [jnp.ones_like(zero)]
    direction = list(resid)
    pressure = [zero] * ITERS
    product = c[0]
    for k in range(ITERS):
        image = list(direction) + [zero]
        for j, value in enumerate(direction):
            if j == 0:
                image[1] = image[1] - value
            else:
                image[j + 1] = image[j + 1] - 0.5 * value
                image[j - 1] = image[j - 1] - 0.5 * value
        bottom = zero
        for i, value in enumerate(direction):
            line = zero
            for j, other in enumerate(image):
                line = line + other * gram(i, j)
            bottom = bottom + value * line
        alpha = ratio(product, bottom)
        for j, value in enumerate(direction):
            pressure[j] = pressure[j] + alpha * value
        if k + 1 < ITERS:
            resid = [a - alpha * b for a, b in zip(resid + [zero], image)]
            following = zero
            for i, value in enumerate(resid):
                line = zero
                for j, other in enumerate(resid):
                    line = line + other * gram(i, j)
                following = following + value * line
            beta = ratio(following, product)
            direction = [a + beta * b for a, b in zip(resid, direction + [zero])]
            product = following

    field = []
    for k in range(3):
        value = pressure[0] * basis[0][k]
        for j in range(1, ITERS):
            value = value + pressure[j] * basis[j][k]
        field.append(value)
    field_e = to_east(field)
    wet = [jnp.where(surface[k], 1.0, 0.0) for k in range(3)]
    wet_e = to_east(wet)
    for h in range(2):
        slope_e = wet[h] * wet_e[h] * (field_e[h] - field[h])
        slope_n = wet[h] * to_north(wet[h]) * (to_north(field[h]) - field[h])
        grad[0, :, 128 * h : 128 * h + 128] = slope_e[0:16]
        grad[1, :, 128 * h : 128 * h + 128] = slope_n[0:16]


def body(lats, lons, tracers, east_velocity, north_velocity, column_levels, surface_term):
    tall = 2 * LEVELS * ROWS
    cells = tracers.reshape(2 * LEVELS, ROWS, 256)
    east = east_velocity.reshape(LEVELS * ROWS, 256)
    north = north_velocity.reshape(LEVELS * ROWS, 256)
    size_a, size_b = lats // NZ, NZ * lons
    vmem = pltpu.VMEM
    scratch = [
        vmem((2, 2, LEVELS * ROWS, 128), BF16),
        vmem((2, 2, LEVELS * ROWS, 128), F32),
        vmem((ROWS, 256), jnp.int32),
        vmem((ROWS, 256), F32),
        vmem((HIGH, 2, 80, 128), F32),
        vmem((HIGH, 2, 80, 128), F32),
        vmem((HIGH, 2, 64, 128), F32),
        vmem((HIGH, 2, 64, 128), F32),
        vmem((HIGH, 2, 2, LEVELS, 128), F32),
        vmem((ROWS, 2, 64, 128), F32),
        vmem((HIGH, 8, 128), F32),
        vmem((HIGH, 8, 128), F32),
        vmem((HIGH, 8, 128), F32),
        vmem((HIGH, 8, 128), F32),
        vmem((ROWS, 8, 128), F32),
        vmem((ROWS, 8, 128), F32),
        vmem((2, 10, 8, 128), F32),
        vmem((2, 9, 8, 128), F32),
        vmem((4, 3, 8, 128), F32),
        vmem((2, 3, 2, 64, 128), BF16),
        vmem((2, 3, 2, 64, 128), BF16),
        vmem((3, 2, 2, LEVELS, 128), BF16),
        vmem((2, 2, 2, LEVELS, 128), BF16),
        vmem((3, 2, 2, LEVELS, 128), BF16),
        vmem((2, 2, 2, LEVELS, 128), BF16),
        vmem((2, 2, 2, 8, 128), F32),
        vmem((2, 2, 8, 128), F32),
        vmem((2, 2, 8, 128), F32),
        vmem((2, 2, 8, 128), F32),
        vmem((2, 8, 128), F32),
        vmem((2, 8, 128), F32),
        vmem((2, 8, 128), F32),
        vmem((2, 8, 128), F32),
        vmem((4, 8, 128), F32),
        vmem((2, 3, HIGH, 128), F32),
        vmem((ROWS, 2, 8, 128), F32),
        vmem((2, tall, 128), F32),
        vmem((1, 128), F32),
        vmem((size_a, 1, 128), F32),
        vmem((1, 128), F32),
        vmem((size_b, 1, 128), F32),
        pltpu.SemaphoreType.DMA((6 + 2 * ROWS,)),
        pltpu.SemaphoreType.DMA((15,)),
        pltpu.SemaphoreType.DMA((15,)),
        pltpu.SemaphoreType.DMA((8,)),
        pltpu.SemaphoreType.DMA((8,)),
        pltpu.SemaphoreType.DMA((size_a,)),
        pltpu.SemaphoreType.DMA((size_a,)),
        pltpu.SemaphoreType.DMA((size_b,)),
        pltpu.SemaphoreType.DMA((size_b,)),
    ]
    hbm, near = pl.BlockSpec(memory_space=pltpu.HBM), pl.BlockSpec(memory_space=pltpu.VMEM)
    updated, gradient = pl.pallas_call(
        functools.partial(kernel, lats, lons),
        out_shape=(pltpu.VMEM((tall, 256), F32), pltpu.VMEM((2, ROWS, 256), F32)),
        in_specs=[hbm] * 5,
        out_specs=(near, near),
        scratch_shapes=scratch,
        compiler_params=pltpu.CompilerParams(
            collective_id=0, has_side_effects=True, vmem_limit_bytes=40 * 1024 * 1024
        ),
    )(*[pltpu.with_memory_space_constraint(x, pltpu.HBM) for x in (cells, east, north, column_levels, surface_term)])
    return updated.reshape(2, LEVELS, ROWS, 256), gradient


def solution(mesh):
    in_specs = (
        P(None, None, "lat", "lon"),
        P(None, "lat", "lon"),
        P(None, "lat", "lon"),
        P("lat", "lon"),
        P("lat", "lon"),
    )
    out_specs = (P(None, None, "lat", "lon"), P(None, "lat", "lon"))
    step = functools.partial(body, mesh.shape["lat"], mesh.shape["lon"])
    return jax.shard_map(step, mesh=mesh, in_specs=in_specs, out_specs=out_specs, check_vma=False)
```

time: 61.5 us -> 45.5 us (0.74)
  Pallas kernels: 54.5 us -> 43.1 us
  local copies, waits for them, and re-layouts: 6.14 us -> 1.59 us
    pallas_call x1, Pallas kernels: 54.5 us -> 43.1 us  [body(): pl.pallas_call(functools.partial(kernel, lats, lons), out_shape=(pltpu.VM...]
    unnamed x12 -> x2, local copies, waits for them, and re-layouts: 6.14 us -> 1.59 us
where the time goes in v2:
time: 45.5 us; the launch traced here: 45.3 us
  Pallas kernels  43.1 us (95%)
  local copies, waits for them, and re-layouts  1.59 us (3%)
  between operations  0.64 us (1%)
    pallas_call x1, Pallas kernels, body(): pl.pallas_call(functools.partial(kernel, lats, lons), out_shape=(pltpu.VM...  43.1 us
    unnamed x2, local copies, waits for them, and re-layouts  1.59 us

profile of v2, /device:TPU:1, one launch (start us, length us, event | category | flops | bytes accessed | tf_op | source)
XLA Modules:
  0.0 45.3 jit_solution(622680220083110191)
XLA Ops:
  0.6 43.1 %shard_map.68 = (f32[1024,256]{1,0:T(8,128)S(1)}, f32[2,16,256]{2,1,0:T(8,128)S(1)}) custom-call(f32[64,16,256]{2,1,0:T(8,128)} %bitcast.5, bf16[512,256]{1,0:T(8,128)(2,1)} %bitcast.6, bf16[512,256]{1,0:T(8,128)(2,1)} %bitcast.7, s32[16,256]{1,0:T(8,128)} %levels_in.1, f32[16,256]{1,0:T(8,128)} %term_in.1), custom_call_target="tpu_custom_call" | custom-call | tf_op jit(solution)/shard_map/pallas_call | solution.py:729
  43.7 1.0 %copy.9 = f32[2,32,16,256]{3,2,1,0:T(8,128)} copy(f32[2,32,16,256]{3,2,1,0:T(8,128)S(1)} %bitcast.4) | data formatting | bytes 2097152
  44.7 0.6 %copy.10 = f32[2,16,256]{2,1,0:T(8,128)} copy(f32[2,16,256]{2,1,0:T(8,128)S(1)} %get-tuple-element.7) | data formatting | bytes 65536

commit v3 on v2

--- a/solution.py
+++ b/solution.py
@@ -31,7 +31,7 @@
 
 def kernel(
     lats, lons, trc, vel_e, vel_n, levels_in, term_in, out, grad,
-    vin, vf, levi, termi, X, M, LP, SX, V, U, Xs, Ms, Us, Vs, Qt, Qv, pack, pack_in, corner_in,
+    vin, vf, levi, termi, X, M, LP, SX, GC, V, U, Xs, Ms, Us, Vs, Qt, Qv, pack, pack_in, corner_in,
     xb, xb_in, vbn, vbs, vbn_in, vbs_in, FL, FT, ft_in,
     FO, gn, gs, ge, gw, gc, MK, FS, tout, sa, ra, sb, rb,
     in_sem, s1, r1, s2, r2, sas, sar, sbs, sbr,
@@ -45,13 +45,36 @@
     size_a, size_b = ny * NX, NZ * lons
     me_a, me_b = y * NX + xx, zz * lons + lo
 
+    def turns(value, count):
+        return [value] + [jnp.where(value + d >= count, value + d - count, value + d) for d in range(1, count)]
+
+    xs, ys, zs, ls = turns(xx, NX), turns(y, ny), turns(zz, NZ), turns(lo, lons)
+
     def partner_a(k):
-        a = lax.rem(me_a + k, size_a)
-        return ((a // NX) * NZ + zz) * NX + lax.rem(a, NX), lo
+        y_k, x_k = ys[k // NX], xs[k % NX]
+        return ((y_k * NZ + zz) * NX + x_k, lo), y_k * NX + x_k
 
     def partner_b(k):
-        b = lax.rem(me_b + k, size_b)
-        return (y * NZ + b // lons) * NX + xx, lax.rem(b, lons)
+        z_k, l_k = zs[k // lons], ls[k % lons]
+        return ((y * NZ + z_k) * NX + xx, l_k), z_k * lons + l_k
+
+    barrier = pltpu.get_barrier_semaphore()
+    around = [
+        (north, east), (south, east), (north, west), (south, west),
+        (north, lo), (south, lo), (la, east), (la, west),
+    ]
+    def ring(d, count):
+        return min(d, count - d)
+
+    far_a = sorted(range(1, size_a), key=lambda k: -ring(k // NX, ny) - ring(k % NX, NX))
+    far_b = sorted(range(1, size_b), key=lambda k: -ring(k % lons, lons) - 0.5 * (k // lons))
+    partners = [partner_a(k)[0] for k in far_a] + [partner_b(k)[0] for k in far_b]
+
+    def greet(devices):
+        for device in devices:
+            pl.semaphore_signal(barrier, inc=1, device_id=device, device_id_type=MESH)
+
+    greet(around)
 
     loads = [
         pltpu.make_async_copy(levels_in, levi, in_sem.at[0]),
@@ -78,15 +101,7 @@
     y_loads = load_rows(inner_rows)
     for load in loads + x_loads + v_loads + y_loads:
         load.start()
-
-    barrier = pltpu.get_barrier_semaphore()
-    around = [
-        (north, lo), (south, lo), (la, east), (la, west),
-        (north, east), (south, east), (north, west), (south, west),
-    ]
-    partners = [partner_a(k) for k in range(1, size_a)] + [partner_b(k) for k in range(1, size_b)]
-    for device in around + partners:
-        pl.semaphore_signal(barrier, inc=1, device_id=device, device_id_type=MESH)
+    greet(partners)
 
     def send(src, dst, k, device, ss=s1, rr=r1):
         copy = pltpu.make_async_remote_copy(
@@ -100,11 +115,13 @@
     lane16 = lax.rem(lane, 16)
     laneq = lane // 16
 
-    def row_pairs(first, last, step, carry=0):
-        def pair(n, carry):
-            return step(first + 2 * n + 1, step(first + 2 * n, carry))
-
-        return lax.fori_loop(0, (last - first) // 2, pair, carry)
+    def rows_of(first, last, step, carry=0, size=2):
+        def group(n, carry):
+            for r in range(size):
+                carry = step(first + size * n + r, carry)
+            return carry
+
+        return lax.fori_loop(0, (last - first) // size, group, carry)
 
     for load in loads:
         load.wait()
@@ -151,7 +168,7 @@
                 V[i, w, h] = vf[w, h, pl.ds(i - HALO, 32, stride=ROWS), :]
         return carry
 
-    row_pairs(HALO, HALO + ROWS, fill_v)
+    rows_of(HALO, HALO + ROWS, fill_v, size=4)
     for j in range(3):
         vbn[j] = V[17 + j].astype(BF16)
     for j in range(2):
@@ -182,7 +199,7 @@
 
     for load in y_loads:
         load.wait()
-    row_pairs(HALO, HALO + ROWS, pack_rows)
+    rows_of(HALO, HALO + ROWS, pack_rows, size=8)
     for a in range(4):
         for w, Q in enumerate((Qt, Qv)):
             for side in range(2):
@@ -249,97 +266,136 @@
     dry = jnp.zeros((8, 128), F32)
     put_masks([jnp.concatenate([FL[h, 0, 0], FL[h, 1, 0], dry], axis=0) for h in range(2)] + [jnp.zeros((24, 128), F32)])
 
-    level = iota((LEVELS, 128), 0).astype(F32)
-    lane_f = iota((LEVELS, 128), 1)
+    level = sub.astype(F32)
     mixing = time_step * biharm_coef
     lifting = time_step * vertical_coef
-    places = [(t, h) for t in range(2) for h in range(2)]
 
     def mask_row(h, n, i):
         return MK[h, n, pl.ds(jnp.where(i >= HALO, i - HALO, i + 20), 1), :]
 
-    def at(ref, i, h, t, up=0):
-        return ref[i, h, 8 + 32 * t + up : 40 + 32 * t + up, :]
-
-    def bare(ref, i, h, t):
-        return ref[i, h, 32 * t : 32 * t + 32, :]
+    def at(ref, i, h, t, g, up=0):
+        start = 8 + 32 * t + 8 * g + up
+        return ref[i, h, start : start + 8, :]
+
+    def bare(t, g):
+        return slice(32 * t + 8 * g, 32 * t + 8 * g + 8)
 
     def shift_e(halves):
         low, high = pltpu.roll(halves[0], 127, 1), pltpu.roll(halves[1], 127, 1)
-        return [jnp.where(lane_f == 127, high, low), high]
+        return [jnp.where(lane == 127, high, low), high]
 
     def shift_w(halves):
         low, high = pltpu.roll(halves[0], 1, 1), pltpu.roll(halves[1], 1, 1)
-        return [low, jnp.where(lane_f == 0, low, high)]
-
-    def north_step(ref, i):
-        wet = [level < mask_row(h, 2, i) for h in range(2)]
-        return [jnp.where(wet[h], at(ref, i + 1, h, t) - at(ref, i, h, t), 0.0) for t, h in places]
-
-    def laplace(ref, first, last):
-        def step(i, below):
-            above = north_step(ref, i)
-            wet = [level < mask_row(h, 1, i) for h in range(2)]
-            for t in range(2):
-                x = [at(ref, i, h, t) for h in range(2)]
-                xe = shift_e(x)
-                flux = []
-                for h in range(2):
-                    SX[i, h, 32 * t : 32 * t + 32, :] = x[h] + xe[h]
-                    flux.append(jnp.where(wet[h], xe[h] - x[h], 0.0))
-                flux_w = shift_w(flux)
-                for h in range(2):
-                    total = (flux[h] - flux_w[h]) + (above[2 * t + h] - below[2 * t + h])
-                    LP[i, h, 32 * t : 32 * t + 32, :] = mixing * total
-            return above
-
-        row_pairs(first, last, step, north_step(ref, first - 1))
-
-    def north_flux(ref, i):
-        flux = []
-        wet = [level < mask_row(h, 2, i) for h in range(2)]
-        for t, h in places:
-            value = V[i, 1, h] * (at(ref, i, h, t) + at(ref, i + 1, h, t))
-            value += bare(LP, i + 1, h, t) - bare(LP, i, h, t)
-            flux.append(jnp.where(wet[h], value, 0.0))
-        return flux
-
-    def tendency(ref, first, last, put):
-        def step(i, below):
-            above = north_flux(ref, i)
-            wet_e = [level < mask_row(h, 1, i) for h in range(2)]
-            deep = [mask_row(h, 0, i) for h in range(2)]
-            wet_u = [level + 1.0 < deep[h] for h in range(2)]
-            wet_d = [jnp.logical_and(level > 0.0, level < deep[h]) for h in range(2)]
-            results = []
-            for t in range(2):
-                lap = [bare(LP, i, h, t) for h in range(2)]
-                lape = shift_e(lap)
-                flux = []
-                for h in range(2):
-                    value = V[i, 0, h] * bare(SX, i, h, t) + (lape[h] - lap[h])
-                    flux.append(jnp.where(wet_e[h], value, 0.0))
-                flux_w = shift_w(flux)
-                for h in range(2):
-                    x = at(ref, i, h, t)
-                    up = jnp.where(wet_u[h], at(ref, i, h, t, 1) - x, 0.0)
-                    down = jnp.where(wet_d[h], x - at(ref, i, h, t, -1), 0.0)
-                    total = (flux_w[h] - flux[h]) + (below[2 * t + h] - above[2 * t + h])
-                    results.append((x, total + lifting * (up - down)))
-            put(i, results)
-            return above
-
-        row_pairs(first, last, step, north_flux(ref, first - 1))
-
-    def put_middle(i, results):
-        for (t, h), (x, half) in zip(places, results):
-            M[i, h, 8 + 32 * t : 40 + 32 * t, :] = x + half
+        return [low, jnp.where(lane == 0, low, high)]
+
+    def pull(rims, q):
+        return None if rims is None else pltpu.roll(rims, (124 - 16 * q) % 128, 1)
+
+    def laplace(ref, firsts, count, size=2):
+        def group(ref, i):
+            edge_e = [[mask_row(h, 1, i + r) for h in range(2)] for r in range(size)]
+            edge_n = [[mask_row(h, 2, i + r) for h in range(2)] for r in range(-1, size)]
+            for g in range(4):
+                here = level + 8.0 * g
+                wet_e = [[here < edge for edge in pair] for pair in edge_e]
+                wet_n = [[here < edge for edge in pair] for pair in edge_n]
+                for t in range(2):
+                    x = [[at(ref, i + r, h, t, g) for h in range(2)] for r in range(-1, size + 1)]
+                    north_flux = [
+                        [jnp.where(wet_n[r][h], x[r + 1][h] - x[r][h], 0.0) for h in range(2)]
+                        for r in range(size + 1)
+                    ]
+                    for r in range(size):
+                        mid = x[r + 1]
+                        xe = shift_e(mid)
+                        flux = [jnp.where(wet_e[r][h], xe[h] - mid[h], 0.0) for h in range(2)]
+                        flux_w = shift_w(flux)
+                        for h in range(2):
+                            SX[i + r, h, bare(t, g), :] = mid[h] + xe[h]
+                            total = (flux[h] - flux_w[h]) + (north_flux[r + 1][h] - north_flux[r][h])
+                            LP[i + r, h, bare(t, g), :] = mixing * total
+
+        def step(n, carry):
+            for first in firsts:
+                group(ref, first + size * n)
+            return carry
+
+        lax.fori_loop(0, count // size, step, 0)
+
+    def northward(ref, i, wet, x, xn, lap, lapn, h, g):
+        value = V[i, 1, h, 8 * g : 8 * g + 8, :] * (x + xn) + (lapn - lap)
+        return jnp.where(wet, value, 0.0)
+
+    def tendency(ref, firsts, count, put, finish, begin=lambda i: None, size=2):
+        for block, first in enumerate(firsts):
+            edge = [mask_row(h, 2, first - 1) for h in range(2)]
+            for g in range(4):
+                for t in range(2):
+                    for h in range(2):
+                        GC[block, h, bare(t, g), :] = northward(
+                            ref, first - 1, level + 8.0 * g < edge[h],
+                            at(ref, first - 1, h, t, g), at(ref, first, h, t, g),
+                            LP[first - 1, h, bare(t, g), :], LP[first, h, bare(t, g), :], h, g,
+                        )
+
+        def group(block, i):
+            deep, edge_e, edge_n = [
+                [[mask_row(h, k, i + r) for h in range(2)] for r in range(size)] for k in range(3)
+            ]
+            done = [[None, None] for _ in range(size)]
+            rims = [begin(i + r) for r in range(size)]
+            for g in range(4):
+                here = level + 8.0 * g
+                for t in range(2):
+                    x = [[at(ref, i + r, h, t, g) for h in range(2)] for r in range(size + 1)]
+                    lap = [[LP[i + r, h, bare(t, g), :] for h in range(2)] for r in range(size + 1)]
+                    below = [GC[block, h, bare(t, g), :] for h in range(2)]
+                    for r in range(size):
+                        pulled = pull(rims[r], 4 * t + g)
+                        lape = shift_e(lap[r])
+                        flux = []
+                        for h in range(2):
+                            value = V[i + r, 0, h, 8 * g : 8 * g + 8, :] * SX[i + r, h, bare(t, g), :]
+                            value += lape[h] - lap[r][h]
+                            flux.append(jnp.where(here < edge_e[r][h], value, 0.0))
+                        flux_w = shift_w(flux)
+                        for h in range(2):
+                            mid = x[r][h]
+                            above = northward(
+                                ref, i + r, here < edge_n[r][h], mid, x[r + 1][h], lap[r][h], lap[r + 1][h], h, g
+                            )
+                            total = (flux_w[h] - flux[h]) + (below[h] - above)
+                            below[h] = above
+                            up = jnp.where(here + 1.0 < deep[r][h], at(ref, i + r, h, t, g, 1) - mid, 0.0)
+                            wet_d = here < deep[r][h]
+                            if g == 0:
+                                wet_d = jnp.logical_and(wet_d, sub > 0)
+                            down = jnp.where(wet_d, mid - at(ref, i + r, h, t, g, -1), 0.0)
+                            part = put(i + r, t, g, h, mid, total + lifting * (up - down), deep[r][h], pulled)
+                            if part is not None:
+                                done[r][h] = part if done[r][h] is None else done[r][h] + part
+                    for h in range(2):
+                        GC[block, h, bare(t, g), :] = below[h]
+            for r in range(size):
+                finish(i + r, done[r])
+
+        def step(n, carry):
+            for block, first in enumerate(firsts):
+                group(block, first + size * n)
+            return carry
+
+        lax.fori_loop(0, count // size, step, 0)
+
+    def put_middle(i, t, g, h, x, half, deep, pulled):
+        M[i, h, 8 + 32 * t + 8 * g : 16 + 32 * t + 8 * g, :] = x + half
+
+    def nothing(i, done):
+        pass
 
     def rim(value):
         return jnp.where(lane16 < 4, value, pltpu.roll(value, 120, 1))
 
-    def patched(value, rims, q, h):
-        pulled = pltpu.roll(rims, (124 - 16 * q) % 128, 1)
+    def patched(value, pulled, h):
         return jnp.where(lane < 2, pulled, value) if h == 0 else jnp.where(lane >= 126, pulled, value)
 
     def patch_middle(i, carry):
@@ -347,7 +403,8 @@
         rims = rim(value)
         parts = []
         for q in range(8):
-            pair = [patched(M[i, h, 8 * q + 8 : 8 * q + 16, :], rims, q, h) for h in range(2)]
+            pulled = pull(rims, q)
+            pair = [patched(M[i, h, 8 * q + 8 : 8 * q + 16, :], pulled, h) for h in range(2)]
             for h in range(2):
                 M[i, h, 8 * q + 8 : 8 * q + 16, :] = pair[h]
             parts.append(tuple(pair))
@@ -356,20 +413,15 @@
         Ms[i] = jnp.where(jnp.logical_and(lane16 >= 4, lane16 < 12), value, own)
         return carry
 
-    def put_updated(i, results):
-        rims = rim(Xs[i])
-        wet = [level < mask_row(h, 0, i) for h in range(2)]
-        sums = [[], []]
-        for (t, h), (m, half) in zip(places, results):
-            value = 0.5 * ((at(X, i, h, t) + m) + half)
-            value = jnp.concatenate(
-                [patched(value[8 * g : 8 * g + 8], rims, 4 * t + g, h) for g in range(4)], axis=0
-            )
-            U[i - HALO, h, 32 * t : 32 * t + 32, :] = value
-            part = jnp.where(wet[h], value, 0.0)
-            sums[t].append((part[0:8] + part[8:16]) + (part[16:24] + part[24:32]))
+    def put_updated(i, t, g, h, m, half, deep, pulled):
+        value = patched(0.5 * ((at(X, i, h, t, g) + m) + half), pulled, h)
+        U[i - HALO, h, bare(t, g), :] = value
+        part = jnp.where(level + 8.0 * g < deep, value, 0.0)
+        return part if t == 0 else -0.5 * part
+
+    def put_forcing(i, done):
         for h in range(2):
-            FS[i - HALO, h] = sums[0][h] - 0.5 * sums[1][h]
+            FS[i - HALO, h] = done[h]
 
     def seam_row(own, from_east, from_west, n):
         value = jnp.where(lane16 < 4, own, pltpu.roll(own, 8, 1))
@@ -430,8 +482,8 @@
         m, half = seam_tendency(Ms, first, last, masks)
         Xs[first:last] = 0.5 * ((Xs[first:last] + m) + half)
 
-    laplace(X, 5, 19)
-    tendency(X, 6, 18, put_middle)
+    laplace(X, [5], 14)
+    tendency(X, [6], 12, put_middle, nothing)
 
     for copy in c_side:
         copy.wait()
@@ -451,65 +503,64 @@
         inside[f].append(jnp.concatenate([beside(f, tile, pack_in[1, 0], pack_in[0, 0]) for tile in range(2)], axis=0))
     masks = seam_masks(inside[0], range(16))
     seam_middle(6, 18, masks)
-    row_pairs(6, 18, patch_middle)
+    rows_of(6, 18, patch_middle, size=6)
     seam_updated(8, 16, part_of(masks, 2, 14))
-    laplace(M, 7, 17)
-    tendency(M, 8, 16, put_updated)
-
-    for copy in c_far:
+    laplace(M, [7], 10)
+    tendency(M, [8], 8, put_updated, put_forcing, lambda i: rim(Xs[i]))
+
+    for copy in c_far[4:6]:
+        copy.wait()
+    no_north = (sub < 4).astype(jnp.int32) * (la == lats - 1).astype(jnp.int32)
+    no_south = (sub >= 4).astype(jnp.int32) * (la == 0).astype(jnp.int32)
+    outside = (no_north + no_south) > 0
+    rims = [[], []]
+    for h in range(2):
+        from_north, from_south = ft_in[1, h], ft_in[0, h]
+        rims[0].append(jnp.where(outside, 0.0, jnp.where(sub < 4, from_north, pltpu.roll(from_south, 4, 0))))
+        rims[1].append(jnp.where(sub < 4, pltpu.roll(from_north, 4, 0), from_south))
+    depth = [jnp.concatenate([inside[0][h], rims[0][h]], axis=0) for h in range(2)]
+    put_masks(depth + [jnp.zeros((24, 128), F32)])
+    for copy in c_far[6:10]:
         copy.wait()
     for j in range(3):
         X[j, :, 8:72, :] = xb_in[0, j].astype(F32)
         X[21 + j, :, 8:72, :] = xb_in[1, j].astype(F32)
+    laplace(X, [1, 19], 4)
+    for copy in c_far[10:]:
+        copy.wait()
     for j in range(2):
         V[2 + j] = vbn_in[1 + j].astype(F32)
         V[20 + j] = vbs_in[j].astype(F32)
     V[1, 1] = vbn_in[0, 1].astype(F32)
-
-    rims = []
+    tendency(X, [2, 18], 4, put_middle, nothing)
+
+    for copy in c_far[:4]:
+        copy.wait()
     for f in range(2):
-        rim_f = []
-        for h in range(2):
-            from_north, from_south = ft_in[1, h], ft_in[0, h]
-            if f == 0:
-                rim_f.append(jnp.where(sub < 4, from_north, pltpu.roll(from_south, 4, 0)))
-            else:
-                rim_f.append(jnp.where(sub < 4, pltpu.roll(from_north, 4, 0), from_south))
         above = beside(f, 0, corner_in[3, 0], corner_in[1, 0])
         below = beside(f, 1, corner_in[2, 2], corner_in[0, 2])
-        rim_f.append(jnp.where(sub < 4, above, below))
-        rims.append(rim_f)
-    no_north = (sub < 4).astype(jnp.int32) * (la == lats - 1).astype(jnp.int32)
-    no_south = (sub >= 4).astype(jnp.int32) * (la == 0).astype(jnp.int32)
-    outside = (no_north + no_south) > 0
-    rims[0] = [jnp.where(outside, 0.0, p) for p in rims[0]]
-    depth = [jnp.concatenate([inside[0][k], rims[0][k]], axis=0) for k in range(3)]
+        rims[f].append(jnp.where(sub < 4, above, below))
+    rims[0][2] = jnp.where(outside, 0.0, rims[0][2])
+    depth.append(jnp.concatenate([inside[0][2], rims[0][2]], axis=0))
     diagonal = [6.0 + jnp.concatenate([inside[1][k], rims[1][k]], axis=0) for k in range(3)]
-    put_masks(depth)
-
-    for first in (1, 19):
-        laplace(X, first, first + 4)
-    for first in (2, 18):
-        tendency(X, first, first + 4, put_middle)
     for n in range(4):
         Xs[n] = seam_row(seam_x(n), corner_in[2, 0], corner_in[0, 0], n)
         Xs[20 + n] = seam_row(seam_x(20 + n), corner_in[3, 1], corner_in[1, 1], n)
-        if n > 0:
-            put_velocity(n, seam_row(seam_v(n), corner_in[2, 1], corner_in[0, 1], n))
-        if n < 2:
-            put_velocity(20 + n, seam_row(seam_v(20 + n), corner_in[3, 2], corner_in[1, 2], n))
+    for n in range(1, 4):
+        put_velocity(n, seam_row(seam_v(n), corner_in[2, 1], corner_in[0, 1], n))
+    for n in range(2):
+        put_velocity(20 + n, seam_row(seam_v(20 + n), corner_in[3, 2], corner_in[1, 2], n))
     masks_low = seam_masks(depth, list(range(20, 24)) + list(range(6)))
     masks_high = seam_masks(depth, range(10, 20))
     seam_middle(2, 6, part_of(masks_low, 0, 8))
     seam_middle(18, 22, part_of(masks_high, 2, 10))
-    row_pairs(2, 6, patch_middle)
-    row_pairs(18, 22, patch_middle)
+    for first in (2, 18):
+        for r in range(4):
+            patch_middle(first + r, 0)
     seam_updated(4, 8, part_of(masks_low, 2, 10))
     seam_updated(16, 20, part_of(masks_high, 0, 8))
-    laplace(M, 3, 7)
-    laplace(M, 17, 21)
-    tendency(M, 4, 8, put_updated)
-    tendency(M, 16, 20, put_updated)
+    laplace(M, [3, 17], 4)
+    tendency(M, [4, 16], 4, put_updated, put_forcing, lambda i: rim(Xs[i]))
 
     def forcing_rows(first, last, h):
         return jnp.sum(FS[first:last, h], axis=1) * (1.0 / math.sqrt(LEVELS))
@@ -542,7 +593,7 @@
             out[rows, 128 * h : 128 * h + 128] = tout[h, rows, :]
         return carry
 
-    row_pairs(0, ROWS, put_rows)
+    rows_of(0, ROWS, put_rows)
     lax.fori_loop(0, 8, put_out, 0)
     row = iota((24, 128), 0)
     surface = [p > 0.0 for p in depth]
@@ -582,30 +633,31 @@
     sums = jnp.sum(jnp.concatenate(rows, axis=0), axis=1, keepdims=True)
     sa[...] = jnp.sum(jnp.where(lane == sub, sums, 0.0), axis=0, keepdims=True)
 
-    def gather(src, dst, me, size, partner, ss, rr):
+    def gather(src, dst, me, size, order, partner, ss, rr):
         copies = []
-        for k in range(1, size):
+        for k in order:
+            device, place = partner(k)
             copy = pltpu.make_async_remote_copy(
                 src_ref=src, dst_ref=dst.at[me], send_sem=ss.at[k], recv_sem=rr.at[me],
-                device_id=partner(k), device_id_type=MESH,
+                device_id=device, device_id_type=MESH,
             )
             copy.start()
-            copies.append(copy)
+            arrival = pltpu.make_async_remote_copy(
+                src_ref=src, dst_ref=dst.at[place], send_sem=ss.at[k], recv_sem=rr.at[place],
+                device_id=device, device_id_type=MESH,
+            )
+            copies.append((copy, arrival))
         dst[me] = src[...]
-        for k in range(1, size):
-            copies[k - 1].wait_send()
-            other = lax.rem(me + k, size)
-            pltpu.make_async_remote_copy(
-                src_ref=src, dst_ref=dst.at[other], send_sem=ss.at[k], recv_sem=rr.at[other],
-                device_id=partner(k), device_id_type=MESH,
-            ).wait_recv()
+        for copy, arrival in copies:
+            copy.wait_send()
+            arrival.wait_recv()
         parts = [dst[k] for k in range(size)]
         while len(parts) > 1:
             parts = [parts[k] + parts[k + 1] for k in range(0, len(parts) - 1, 2)] + parts[len(parts) - len(parts) % 2 :]
         return parts[0]
 
-    sb[...] = gather(sa, ra, me_a, size_a, partner_a, sas, sar)
-    total = gather(sb, rb, me_b, size_b, partner_b, sbs, sbr)
+    sb[...] = gather(sa, ra, me_a, size_a, far_a, partner_a, sas, sar)
+    total = gather(sb, rb, me_b, size_b, far_b, partner_b, sbs, sbr)
     inner = [jnp.broadcast_to(total[:, k : k + 1], (1, 128)) for k in range(8)]
     c = inner[:2] + [2.0 * inner[k] - inner[k % 2] for k in range(2, 8)]
 
@@ -682,6 +734,7 @@
         vmem((HIGH, 2, 80, 128), F32),
         vmem((HIGH, 2, 64, 128), F32),
         vmem((HIGH, 2, 64, 128), F32),
+        vmem((2, 2, 64, 128), F32),
         vmem((HIGH, 2, 2, LEVELS, 128), F32),
         vmem((ROWS, 2, 64, 128), F32),
         vmem((HIGH, 8, 128), F32),

time: 45.5 us -> 43 us (0.945)
  Pallas kernels: 43.1 us -> 40.6 us
    pallas_call x1, Pallas kernels: 43.1 us -> 40.6 us  [body(): pl.pallas_call(functools.partial(kernel, lats, lons), out_shape=(pltpu.VM...]
where the time goes in v3:
time: 43 us; the launch traced here: 42.8 us
  Pallas kernels  40.6 us (94%)
  local copies, waits for them, and re-layouts  1.59 us (4%)
  between operations  0.64 us (1%)
    pallas_call x1, Pallas kernels, body(): pl.pallas_call(functools.partial(kernel, lats, lons), out_shape=(pltpu.VM...  40.6 us
    unnamed x2, local copies, waits for them, and re-layouts  1.59 us

profile of v3, /device:TPU:1, one launch (start us, length us, event | category | flops | bytes accessed | tf_op | source)
XLA Modules:
  0.0 42.8 jit_solution(10977777048263239029)
XLA Ops:
  0.6 40.6 %shard_map.68 = (f32[1024,256]{1,0:T(8,128)S(1)}, f32[2,16,256]{2,1,0:T(8,128)S(1)}) custom-call(f32[64,16,256]{2,1,0:T(8,128)} %bitcast.5, bf16[512,256]{1,0:T(8,128)(2,1)} %bitcast.6, bf16[512,256]{1,0:T(8,128)(2,1)} %bitcast.7, s32[16,256]{1,0:T(8,128)} %levels_in.1, f32[16,256]{1,0:T(8,128)} %term_in.1), custom_call_target="tpu_custom_call" | custom-call | tf_op jit(solution)/shard_map/pallas_call | solution.py:782
  41.2 1.0 %copy.9 = f32[2,32,16,256]{3,2,1,0:T(8,128)} copy(f32[2,32,16,256]{3,2,1,0:T(8,128)S(1)} %bitcast.4) | data formatting | bytes 2097152
  42.2 0.6 %copy.10 = f32[2,16,256]{2,1,0:T(8,128)} copy(f32[2,16,256]{2,1,0:T(8,128)S(1)} %get-tuple-element.7) | data formatting | bytes 65536

commit v4 on v3

--- a/solution.py
+++ b/solution.py
@@ -486,7 +486,7 @@
     tendency(X, [6], 12, put_middle, nothing)
 
     for copy in c_side:
-        copy.wait()
+        copy.wait_recv()
     for a in range(4):
         for n in range(4):
             i = HALO + 4 * a + n
@@ -509,7 +509,7 @@
     tendency(M, [8], 8, put_updated, put_forcing, lambda i: rim(Xs[i]))
 
     for copy in c_far[4:6]:
-        copy.wait()
+        copy.wait_recv()
     no_north = (sub < 4).astype(jnp.int32) * (la == lats - 1).astype(jnp.int32)
     no_south = (sub >= 4).astype(jnp.int32) * (la == 0).astype(jnp.int32)
     outside = (no_north + no_south) > 0
@@ -521,21 +521,23 @@
     depth = [jnp.concatenate([inside[0][h], rims[0][h]], axis=0) for h in range(2)]
     put_masks(depth + [jnp.zeros((24, 128), F32)])
     for copy in c_far[6:10]:
-        copy.wait()
+        copy.wait_recv()
     for j in range(3):
         X[j, :, 8:72, :] = xb_in[0, j].astype(F32)
         X[21 + j, :, 8:72, :] = xb_in[1, j].astype(F32)
     laplace(X, [1, 19], 4)
+    rim_x = [(seam_x(n), seam_x(20 + n)) for n in range(4)]
     for copy in c_far[10:]:
-        copy.wait()
+        copy.wait_recv()
     for j in range(2):
         V[2 + j] = vbn_in[1 + j].astype(F32)
         V[20 + j] = vbs_in[j].astype(F32)
     V[1, 1] = vbn_in[0, 1].astype(F32)
     tendency(X, [2, 18], 4, put_middle, nothing)
+    rim_v = [seam_v(n) for n in (1, 2, 3, 20, 21)]
 
     for copy in c_far[:4]:
-        copy.wait()
+        copy.wait_recv()
     for f in range(2):
         above = beside(f, 0, corner_in[3, 0], corner_in[1, 0])
         below = beside(f, 1, corner_in[2, 2], corner_in[0, 2])
@@ -544,12 +546,12 @@
     depth.append(jnp.concatenate([inside[0][2], rims[0][2]], axis=0))
     diagonal = [6.0 + jnp.concatenate([inside[1][k], rims[1][k]], axis=0) for k in range(3)]
     for n in range(4):
-        Xs[n] = seam_row(seam_x(n), corner_in[2, 0], corner_in[0, 0], n)
-        Xs[20 + n] = seam_row(seam_x(20 + n), corner_in[3, 1], corner_in[1, 1], n)
+        Xs[n] = seam_row(rim_x[n][0], corner_in[2, 0], corner_in[0, 0], n)
+        Xs[20 + n] = seam_row(rim_x[n][1], corner_in[3, 1], corner_in[1, 1], n)
     for n in range(1, 4):
-        put_velocity(n, seam_row(seam_v(n), corner_in[2, 1], corner_in[0, 1], n))
+        put_velocity(n, seam_row(rim_v[n - 1], corner_in[2, 1], corner_in[0, 1], n))
     for n in range(2):
-        put_velocity(20 + n, seam_row(seam_v(20 + n), corner_in[3, 2], corner_in[1, 2], n))
+        put_velocity(20 + n, seam_row(rim_v[3 + n], corner_in[3, 2], corner_in[1, 2], n))
     masks_low = seam_masks(depth, list(range(20, 24)) + list(range(6)))
     masks_high = seam_masks(depth, range(10, 20))
     seam_middle(2, 6, part_of(masks_low, 0, 8))
@@ -600,7 +602,7 @@
     inverse = [jnp.where(surface[k], 1.0 / diagonal[k], 0.0) for k in range(3)]
     weight = [jnp.where(row < 16, diagonal[k], 0.0) for k in range(2)]
     for copy in c_forcing:
-        copy.wait()
+        copy.wait_recv()
     forcing = flat(
         [[FO[h, tile] for tile in range(2)] for h in range(2)],
         [gn[h] for h in range(2)], [gs[h] for h in range(2)],
@@ -632,6 +634,8 @@
         rows.append(partial(weighted, basis[j + 1]))
     sums = jnp.sum(jnp.concatenate(rows, axis=0), axis=1, keepdims=True)
     sa[...] = jnp.sum(jnp.where(lane == sub, sums, 0.0), axis=0, keepdims=True)
+
+    sent = c_side + c_far + c_forcing
 
     def gather(src, dst, me, size, order, partner, ss, rr):
         copies = []
@@ -649,8 +653,8 @@
             copies.append((copy, arrival))
         dst[me] = src[...]
         for copy, arrival in copies:
-            copy.wait_send()
             arrival.wait_recv()
+            sent.append(copy)
         parts = [dst[k] for k in range(size)]
         while len(parts) > 1:
             parts = [parts[k] + parts[k + 1] for k in range(0, len(parts) - 1, 2)] + parts[len(parts) - len(parts) % 2 :]
@@ -716,6 +720,8 @@
         slope_n = wet[h] * to_north(wet[h]) * (to_north(field[h]) - field[h])
         grad[0, :, 128 * h : 128 * h + 128] = slope_e[0:16]
         grad[1, :, 128 * h : 128 * h + 128] = slope_n[0:16]
+    for copy in sent:
+        copy.wait_send()
 
 
 def body(lats, lons, tracers, east_velocity, north_velocity, column_levels, surface_term):
@@ -727,7 +733,7 @@
     vmem = pltpu.VMEM
     scratch = [
         vmem((2, 2, LEVELS * ROWS, 128), BF16),
-        vmem((2, 2, LEVELS * ROWS, 128), F32),
+        vmem((2, 2, LEVELS * ROWS + ROWS, 128), F32),
         vmem((ROWS, 256), jnp.int32),
         vmem((ROWS, 256), F32),
         vmem((HIGH, 2, 80, 128), F32),
@@ -763,7 +769,7 @@
         vmem((4, 8, 128), F32),
         vmem((2, 3, HIGH, 128), F32),
         vmem((ROWS, 2, 8, 128), F32),
-        vmem((2, tall, 128), F32),
+        vmem((2, tall + ROWS, 128), F32),
         vmem((1, 128), F32),
         vmem((size_a, 1, 128), F32),
         vmem((1, 128), F32),

time: 43 us -> 43.1 us (level)
  no operation moved by 1% of the time
where the time goes in v4:
time: 43.1 us; the launch traced here: 43 us
  Pallas kernels  40.8 us (95%)
  local copies, waits for them, and re-layouts  1.59 us (4%)
  between operations  0.64 us (1%)
    pallas_call x1, Pallas kernels, body(): pl.pallas_call(functools.partial(kernel, lats, lons), out_shape=(pltpu.VM...  40.8 us
    unnamed x2, local copies, waits for them, and re-layouts  1.59 us

profile of v4, /device:TPU:1, one launch (start us, length us, event | category | flops | bytes accessed | tf_op | source)
XLA Modules:
  0.0 43.0 jit_solution(8637293025281394311)
XLA Ops:
  0.6 40.8 %shard_map.68 = (f32[1024,256]{1,0:T(8,128)S(1)}, f32[2,16,256]{2,1,0:T(8,128)S(1)}) custom-call(f32[64,16,256]{2,1,0:T(8,128)} %bitcast.5, bf16[512,256]{1,0:T(8,128)(2,1)} %bitcast.6, bf16[512,256]{1,0:T(8,128)(2,1)} %bitcast.7, s32[16,256]{1,0:T(8,128)} %levels_in.1, f32[16,256]{1,0:T(8,128)} %term_in.1), custom_call_target="tpu_custom_call" | custom-call | tf_op jit(solution)/shard_map/pallas_call | solution.py:788
  41.4 1.0 %copy.9 = f32[2,32,16,256]{3,2,1,0:T(8,128)} copy(f32[2,32,16,256]{3,2,1,0:T(8,128)S(1)} %bitcast.4) | data formatting | bytes 2097152
  42.4 0.6 %copy.10 = f32[2,16,256]{2,1,0:T(8,128)} copy(f32[2,16,256]{2,1,0:T(8,128)S(1)} %get-tuple-element.7) | data formatting | bytes 65536

commit v5 on v3

--- a/solution.py
+++ b/solution.py
@@ -75,6 +75,7 @@
             pl.semaphore_signal(barrier, inc=1, device_id=device, device_id_type=MESH)
 
     greet(around)
+    greet(partners)
 
     loads = [
         pltpu.make_async_copy(levels_in, levi, in_sem.at[0]),
@@ -101,8 +102,6 @@
     y_loads = load_rows(inner_rows)
     for load in loads + x_loads + v_loads + y_loads:
         load.start()
-    greet(partners)
-
     def send(src, dst, k, device, ss=s1, rr=r1):
         copy = pltpu.make_async_remote_copy(
             src_ref=src, dst_ref=dst, send_sem=ss.at[k], recv_sem=rr.at[k], device_id=device, device_id_type=MESH

time: 43 us -> 42.9 us (level)
  no operation moved by 1% of the time
where the time goes in v5:
time: 42.9 us; the launch traced here: 42.8 us
  Pallas kernels  40.5 us (94%)
  local copies, waits for them, and re-layouts  1.59 us (4%)
  between operations  0.64 us (1%)
    pallas_call x1, Pallas kernels, body(): pl.pallas_call(functools.partial(kernel, lats, lons), out_shape=(pltpu.VM...  40.5 us
    unnamed x2, local copies, waits for them, and re-layouts  1.59 us

profile of v5, /device:TPU:1, one launch (start us, length us, event | category | flops | bytes accessed | tf_op | source)
XLA Modules:
  0.0 42.8 jit_solution(15852587251513843220)
XLA Ops:
  0.6 40.5 %shard_map.68 = (f32[1024,256]{1,0:T(8,128)S(1)}, f32[2,16,256]{2,1,0:T(8,128)S(1)}) custom-call(f32[64,16,256]{2,1,0:T(8,128)} %bitcast.5, bf16[512,256]{1,0:T(8,128)(2,1)} %bitcast.6, bf16[512,256]{1,0:T(8,128)(2,1)} %bitcast.7, s32[16,256]{1,0:T(8,128)} %levels_in.1, f32[16,256]{1,0:T(8,128)} %term_in.1), custom_call_target="tpu_custom_call" | custom-call | tf_op jit(solution)/shard_map/pallas_call | solution.py:781
  41.2 1.0 %copy.9 = f32[2,32,16,256]{3,2,1,0:T(8,128)} copy(f32[2,32,16,256]{3,2,1,0:T(8,128)S(1)} %bitcast.4) | data formatting | bytes 2097152
  42.2 0.6 %copy.10 = f32[2,16,256]{2,1,0:T(8,128)} copy(f32[2,16,256]{2,1,0:T(8,128)S(1)} %get-tuple-element.7) | data formatting | bytes 65536
